TPU v7x, 32 devices: a whole 2x2x4 slice. The times are simulated.
32 devices in a mesh: orb: 8 (over z, x), grp: 4 (over y, core).
Axes of the slice: x: 2, y: 2, z: 4, core: 2. Of those that a mesh axis runs over, the one named last changes fastest.
Arguments:
- orbitals: float32 [64, 48, 2304], P(('orb', 'grp')), may hold values from -6 to 6
- kernel: float32 [48, 2304], replicated, may hold values from 0.1 to 2
- anchors: int32 [8, 3], replicated, may hold values from 0 to 16
- pair_count: int32 [8], P('orb'), may hold values from 1 to 8, 32 in all
- pair_first: int32 [64], P('orb'), may hold values from 0 to 7
- pair_second: int32 [64], P('orb'), may hold values from 0 to 7
- pair_reach: int32 [64], P('orb'), may hold values from 0 to 2
Outputs:
- gradient: float32 [64, 48, 2304], P('orb', 'grp')
- lagrange: float32 [8, 8, 8], P('orb')
Inputs may be any that keep to these rules, and one draw needn't show every extreme that they name: The live slots of a fragment are its first pair_count slots; some fragment has all 8 live.
All inputs are finite; a program needn't handle non-finite values. No bound on the sum of `pair_count` on one device may be relied on, other than what follows from the above.
Results may differ from a plain program's by a relative error of at most 0.0003.
Values sent between devices are 32-bit elements; how exact they have to be, the bound alone decides.
No kernel may reach another device: no remote copies, remote signals or barrier semaphores. Data moves between devices by JAX's collectives and lax.ppermute only.
A program may use at most 128 MiB of HBM per device.

v0:
```python
import functools
import math

import jax
import jax.numpy as jnp
import numpy as np
from jax import lax
from jax.experimental import pallas as pl
from jax.experimental.pallas import tpu as pltpu
from jax.sharding import PartitionSpec as P

REACH = 2
LANES = 128
ROWS = 8
HALF = LANES // 2


class Number:
    def __init__(self, real, imag=None):
        self.real, self.imag = real, imag

    def __add__(self, other):
        if self.imag is None or other.imag is None:
            imag = self.imag if other.imag is None else other.imag
        else:
            imag = self.imag + other.imag
        return Number(self.real + other.real, imag)

    def __sub__(self, other):
        if other.imag is None:
            imag = self.imag
        else:
            imag = -other.imag if self.imag is None else self.imag - other.imag
        return Number(self.real - other.real, imag)

    def conj(self):
        return self if self.imag is None else Number(self.real, -self.imag)

    def scaled(self, factor):
        return Number(self.real * factor, None if self.imag is None else self.imag * factor)

    def turned(self, sign):
        if self.imag is None:
            return Number(jnp.zeros_like(self.real), self.real if sign > 0 else -self.real)
        return Number(-self.imag, self.real) if sign > 0 else Number(self.imag, -self.real)

    def plus_turned(self, other, sign):
        if sign < 0:
            return self.minus_turned(other)
        real = self.real if other.imag is None else self.real - other.imag
        return Number(real, other.real if self.imag is None else self.imag + other.real)

    def minus_turned(self, other):
        real = self.real if other.imag is None else self.real + other.imag
        return Number(real, -other.real if self.imag is None else self.imag - other.real)

    def times(self, angle):
        real, imag = math.cos(angle), math.sin(angle)
        if abs(imag) < 1e-12:
            return self if real > 0 else self.scaled(-1.0)
        if abs(real) < 1e-12:
            return self.turned(imag)
        if self.imag is None:
            return Number(self.real * real, self.real * imag)
        return Number(self.real * real - self.imag * imag, self.real * imag + self.imag * real)


def coprime(n):
    for p in (2, 3, 5, 7):
        power = 1
        while n % (power * p) == 0:
            power *= p
        if 1 < power < n:
            return power, n // power
    return None


def radix(n):
    return next((p for p in (4, 2, 3, 5, 7) if n % p == 0 and n > p), None)


def meeting(i, j, first, second):
    return next(k for k in range(first * second) if k % first == i and k % second == j)


def dft(values, sign):
    n = len(values)
    if n == 1:
        return values
    if n == 2:
        return [values[0] + values[1], values[0] - values[1]]
    if n == 3:
        a, b, c = values
        total, side = b + c, (b - c).scaled(math.sqrt(0.75))
        middle = a - total.scaled(0.5)
        return [a + total, middle.plus_turned(side, sign), middle.plus_turned(side, -sign)]
    if n == 4:
        a, b, c, d = values
        s, t, u, v = a + c, a - c, b + d, b - d
        return [s + u, t.plus_turned(v, sign), s - u, t.plus_turned(v, -sign)]
    out = [None] * n
    if coprime(n):
        first, second = coprime(n)
        columns = [
            dft([values[(i * second + j * first) % n] for i in range(first)], sign)
            for j in range(second)
        ]
        for i in range(first):
            row = dft([column[i] for column in columns], sign)
            for j in range(second):
                out[meeting(i, j, first, second)] = row[j]
        return out
    p = radix(n)
    if p:
        rest = n // p
        columns = [dft(values[j::p], sign) for j in range(p)]
        for i in range(rest):
            row = dft(
                [columns[j][i].times(sign * 2.0 * math.pi * i * j / n) for j in range(p)], sign
            )
            for j in range(p):
                out[i + rest * j] = row[j]
        return out
    for k in range(n):
        total = values[0]
        for j in range(1, n):
            total = total + values[j].times(sign * 2.0 * math.pi * (j * k % n) / n)
        out[k] = total
    return out


def real_dft(values):
    n = len(values)
    if n <= 4:
        out = dft(values, -1)
    else:
        out = [None] * n
        if coprime(n):
            first, second = coprime(n)
            columns = [
                real_dft([values[(i * second + j * first) % n] for i in range(first)])
                for j in range(second)
            ]
            for i in range(first // 2 + 1):
                entries = [column[i] for column in columns]
                alone = 2 * i % first == 0
                row = real_dft(entries) if alone else dft(entries, -1)
                for j in range(second):
                    out[meeting(i, j, first, second)] = row[j]
        elif radix(n):
            p = radix(n)
            rest = n // p
            columns = [real_dft(values[j::p]) for j in range(p)]
            for i in range(rest // 2 + 1):
                row = dft(
                    [columns[j][i].times(-2.0 * math.pi * i * j / n) for j in range(p)], -1
                )
                for j in range(p):
                    out[i + rest * j] = row[j]
        else:
            out = dft(values, -1)
    for k in range(1, n):
        if out[k] is None or (k > n // 2 and out[n - k] is not None):
            out[k] = out[n - k].conj()
    out[0] = Number(out[0].real)
    if n % 2 == 0:
        out[n // 2] = Number(out[n // 2].real)
    return out


def real_back(values):
    n = len(values)
    if n == 1:
        return [values[0].real]
    if n == 2:
        return [values[0].real + values[1].real, values[0].real - values[1].real]
    if n == 3:
        a, b = values[0].real, values[1]
        side = b.imag * math.sqrt(3.0)
        middle = a - b.real
        return [a + 2.0 * b.real, middle - side, middle + side]
    if n == 4:
        s, t = values[0].real + values[2].real, values[0].real - values[2].real
        u, v = 2.0 * values[1].real, 2.0 * values[1].imag
        return [s + u, t - v, s - u, t + v]
    out = [None] * n
    if coprime(n):
        first, second = coprime(n)
        rows = []
        for i in range(first // 2 + 1):
            entries = [values[meeting(i, j, first, second)] for j in range(second)]
            if 2 * i % first == 0:
                rows.append([Number(value) for value in real_back(entries)])
            else:
                rows.append(dft(entries, 1))
        for b in range(second):
            half = [row[b] for row in rows]
            whole = half + [half[first - i].conj() for i in range(len(half), first)]
            for a, value in enumerate(real_back(whole)):
                out[(a * second + b * first) % n] = value
        return out
    p = radix(n)
    if p:
        rest = n // p
        parts = []
        for i in range(p // 2 + 1):
            entries = values[i::p]
            if i == 0:
                parts.append([Number(value) for value in real_back(entries)])
            else:
                inner = dft(entries, 1)
                parts.append([inner[m].times(2.0 * math.pi * i * m / n) for m in range(rest)])
                if 2 * i == p:
                    parts[-1] = [Number(value.real) for value in parts[-1]]
        for m in range(rest):
            half = [part[m] for part in parts]
            whole = half + [half[p - i].conj() for i in range(len(half), p)]
            for j, value in enumerate(real_back(whole)):
                out[m + rest * j] = value
        return out
    return [value.real for value in dft(values, 1)]


def lane_matrices(edge):
    index = np.arange(edge)
    angles = 2.0 * np.pi / edge * (np.outer(index, index) % edge)
    found = []
    for sign in (-1.0, 1.0):
        full = np.zeros((2, 2, edge, 2, 2, edge))
        for side in range(2):
            full[0, side, :, 0, side] = np.cos(angles)
            full[0, side, :, 1, side] = sign * np.sin(angles)
            full[1, side, :, 0, side] = -sign * np.sin(angles)
            full[1, side, :, 1, side] = np.cos(angles)
        full = np.pad(full, [(0, 0), (0, 0), (0, HALF - edge)] * 2).reshape(2 * LANES, 2 * LANES)
        high = full.astype(jnp.bfloat16)
        low = (full - high.astype(np.float64)).astype(jnp.bfloat16)
        found.append(np.stack([high, low]))
    return found


def split_dot(real, imag, matrix):
    value = jnp.concatenate([real, imag], axis=1)
    high = value.astype(jnp.bfloat16)
    low = (value - high.astype(jnp.float32)).astype(jnp.bfloat16)
    product = jnp.dot(high, matrix[0], preferred_element_type=jnp.float32)
    product += jnp.dot(low, matrix[0], preferred_element_type=jnp.float32)
    product += jnp.dot(high, matrix[1], preferred_element_type=jnp.float32)
    return product[:, :LANES], product[:, LANES:]


def padded_half(edge):
    return -(-(edge // 2 + 1) // ROWS) * ROWS


def screen_kernel(edge, kernel_ref, flip_ref, mirror_ref, out_ref, flipped):
    exact = dict(precision=lax.Precision.HIGHEST, preferred_element_type=jnp.float32)
    flipped[...] = jnp.dot(flip_ref[...], kernel_ref[...], **exact)
    height = padded_half(edge)
    lane = lax.broadcasted_iota(jnp.int32, (edge, LANES), 1)
    out_ref[...] = jnp.zeros_like(out_ref)

    def piece(ref, y):
        begin, offset = divmod(y * edge, LANES)
        value = ref[:, begin * LANES : (begin + 1) * LANES]
        value = pltpu.roll(value, LANES - offset, 1) if offset else value
        if offset + edge > LANES:
            more = ref[:, (begin + 1) * LANES : (begin + 2) * LANES]
            value = jnp.where(lane < LANES - offset, value, pltpu.roll(more, LANES - offset, 1))
        return value

    for y in range(edge // 2 + 1):
        value = piece(kernel_ref, y)
        value = jnp.where(lane < HALF, value, pltpu.roll(value, HALF, 1))
        value = value + jnp.dot(piece(flipped, (edge - y) % edge), mirror_ref[...], **exact)
        value = value * (0.5 / float(edge**3))
        for t in range(edge // ROWS):
            out_ref[pl.ds(t * ROWS * height + y, ROWS, stride=height), :] = value[t * ROWS : (t + 1) * ROWS]


def screen_terms(kernel):
    edge, plane = kernel.shape
    index = np.arange(edge)
    flip = np.zeros((edge, edge), np.float32)
    flip[index, -index % edge] = 1.0
    mirror = np.zeros((LANES, LANES), np.float32)
    mirror[-index % edge, index] = 1.0
    mirror[-index % edge, HALF + index] = 1.0
    vmem = pl.BlockSpec(memory_space=pltpu.VMEM)
    return pl.pallas_call(
        functools.partial(screen_kernel, edge),
        out_shape=jax.ShapeDtypeStruct((edge * padded_half(edge), LANES), jnp.float32),
        in_specs=[vmem] * 3,
        out_specs=vmem,
        scratch_shapes=[pltpu.VMEM((edge, plane), jnp.float32)],
        compiler_params=pltpu.CompilerParams(vmem_limit_bytes=16 << 20),
        name="screen_terms",
    )(kernel, jnp.asarray(flip), jnp.asarray(mirror))


def pair_kernel(
    shape,
    places_ref,
    count_ref,
    first_ref,
    second_ref,
    reach_ref,
    anchors_ref,
    *refs,
):
    edge, orb_dev, groups, fragments, slots = shape
    plane = edge * edge
    chunks = plane // LANES
    tiles = edge // ROWS
    half = edge // 2 + 1
    height = padded_half(edge)
    returns_count = (REACH + 1) * orb_dev
    tables, refs = refs[:4], refs[4:]
    phi_refs, refs = refs[:groups], refs[groups:]
    (twin_ref, relay_ref, one_ref, two_ref), refs = refs[:4], refs[4:]
    act_outs, back_outs, refs = refs[:2], refs[2:6], refs[6:]
    (act, back, near, far, wide, moved, dense, cube, lower, upper, listed, load_sem, out_sem) = refs[:13]
    spots_ref, screen_ref, ahead_ref, behind_ref = refs[13:17]
    table_sem = refs[17]

    fragment = places_ref[0]
    member = places_ref[1]
    table_copies = [
        pltpu.make_async_copy(table, hold, table_sem.at[i])
        for i, (table, hold) in enumerate(zip(tables, refs[13:17]))
    ]
    for copy in table_copies:
        copy.start()
    lane = lax.broadcasted_iota(jnp.int32, (edge, LANES), 1)
    row = lax.broadcasted_iota(jnp.int32, (edge, LANES), 0)
    period = edge * LANES // math.gcd(edge, LANES) // edge
    group_chunks = period * edge // LANES
    stretch = next(n for n in (6, 4, 3, 2, 1) if chunks % n == 0)
    middle = pl.ds(edge, edge)

    def list_slots(slot, found):
        mine = (slot < count_ref[0]) & (lax.div(second_ref[slot], orb_dev) == member)

        @pl.when(mine)
        def _():
            listed[found] = slot

        return found + mine.astype(jnp.int32)

    found = lax.fori_loop(0, slots, list_slots, 0)

    def slot_of(turn, side):
        at = 2 * turn + side
        live = at < found
        return listed[jnp.where(live, at, 2 * turn)], live

    def far_copy(side, source):
        return pltpu.make_async_copy(source, far.at[side], load_sem.at[1, side])

    def start_loads(turn):
        for side in range(2):
            slot, _ = slot_of(turn, side)
            first, second, reach = first_ref[slot], second_ref[slot], reach_ref[slot]
            relative = lax.div(first, orb_dev) ^ member
            for k in range(groups):
                @pl.when(relative == k)
                def _():
                    pltpu.make_async_copy(
                        phi_refs[k].at[lax.rem(first, orb_dev)], near.at[side], load_sem.at[0, side]
                    ).start()
            own = lax.rem(second, orb_dev)

            @pl.when(reach == 0)
            def _():
                far_copy(side, phi_refs[0].at[own]).start()

            @pl.when((reach == 1) & (own == 0) & (lax.rem(fragment, 2) == 0))
            def _():
                far_copy(side, twin_ref.at[0]).start()

            @pl.when((reach == 1) & (own == 0) & (lax.rem(fragment, 2) == 1))
            def _():
                far_copy(side, relay_ref.at[0]).start()

            @pl.when((reach == 1) & (own > 0))
            def _():
                far_copy(side, one_ref.at[jnp.maximum(own - 1, 0)]).start()

            @pl.when(reach == 2)
            def _():
                far_copy(side, two_ref.at[own]).start()

    def wait_loads():
        for side in range(2):
            pltpu.make_async_copy(phi_refs[0].at[0], near.at[side], load_sem.at[0, side]).wait()
            far_copy(side, phi_refs[0].at[0]).wait()

    @pl.when(found > 0)
    def _():
        start_loads(0)

    act[...] = jnp.zeros_like(act)
    back[...] = jnp.zeros_like(back)
    for copy in table_copies:
        copy.wait()

    def offset_of(slot):
        partner = lax.rem(fragment + reach_ref[slot], fragments)
        return [anchors_ref[partner, i] - anchors_ref[fragment, i] for i in range(3)]

    def columns(k):
        return pl.ds(pl.multiple_of(k * LANES, LANES), LANES)

    def shifted(source, delta, k, count):
        shift = lax.rem(delta[1] * edge + delta[2] + 4 * plane, plane)
        start = lax.rem(plane - shift, plane)
        whole, part = lax.div(start, LANES), lax.rem(start, LANES)
        turn = lax.rem(LANES - part, LANES)
        down = edge - jnp.clip(delta[0], -edge, edge)
        x = row - delta[0]
        rows_inside = (x >= 0) & (x < edge)
        pieces = [
            pltpu.roll(source[lax.rem(k + i + whole, chunks), pl.ds(down, edge), :], turn, 1)
            for i in range(count + 1)
        ]
        out = []
        for i in range(count):
            value = jnp.where(lane < LANES - part, pieces[i], pieces[i + 1])
            y = spots_ref[0, pl.ds(k + i, 1), :] - delta[1]
            z = spots_ref[1, pl.ds(k + i, 1), :] - delta[2]
            inside = (y >= 0) & (y < edge) & (z >= 0) & (z < edge)
            out.append(jnp.where(inside & rows_inside, value, 0.0))
        return out

    def solve_two(turn, _):
        @pl.when(turn > 0)
        def _():
            start_loads(turn)

        wait_loads()
        picked = [slot_of(turn, side) for side in range(2)]
        offsets = [offset_of(slot) for slot, _ in picked]
        weights = [live.astype(jnp.float32) for _, live in picked]

        def widen(g, _):
            for side in range(2):
                for i in range(stretch):
                    k = g * stretch + i
                    wide[side, k, middle, :] = far[side, :, columns(k)]
            return 0

        lax.fori_loop(0, chunks // stretch, widen, 0)

        def make_density(g, _):
            for side in range(2):
                values = shifted(wide.at[side], offsets[side], g * stretch, stretch)
                for i, value in enumerate(values):
                    k = g * stretch + i
                    moved[side, k] = value
                    dense[side, k, middle, :] = weights[side] * near[side, :, columns(k)] * value
            return 0

        lax.fori_loop(0, chunks // stretch, make_density, 0)

        def spread(g, _):
            parts = [
                [dense[side, g * group_chunks + q, middle, :] for q in range(group_chunks)]
                for side in range(2)
            ]
            for i in range(period):
                begin, offset = divmod(i * edge, LANES)
                sides = []
                for side in range(2):
                    shift = (side * HALF - offset) % LANES
                    value = parts[side][begin]
                    value = pltpu.roll(value, shift, 1) if shift else value
                    if offset + edge > LANES:
                        more = parts[side][begin + 1]
                        more = pltpu.roll(more, shift, 1) if shift else more
                        value = jnp.where(lane < side * HALF + LANES - offset, value, more)
                    sides.append(value)
                at = pl.multiple_of((g * period + i) * edge, ROWS)
                cube[pl.ds(at, edge), :] = jnp.where(lane < HALF, sides[0], sides[1])
            return 0

        lax.fori_loop(0, edge // period, spread, 0)

        def tile(t, i, size):
            return pl.ds(pl.multiple_of(i * size + t * ROWS, ROWS), ROWS)

        def across(t, i, size):
            return pl.ds(t * (ROWS * size) + i, ROWS, stride=size)

        def over_y(t, _):
            values = real_dft([Number(cube[tile(t, i, edge), :]) for i in range(edge)])
            for i in range(half):
                at = tile(t, i, edge)
                lower[0, at, :] = values[i].real
                lower[1, at, :] = (
                    jnp.zeros((ROWS, LANES), jnp.float32) if values[i].imag is None else values[i].imag
                )
            return 0

        lax.fori_loop(0, tiles, over_y, 0)

        def over_x(t, _):
            at = [across(t, i, edge) for i in range(edge)]
            values = dft([Number(lower[0, a, :], lower[1, a, :]) for a in at], -1)
            for i in range(edge):
                upper[0, tile(t, i, height), :] = values[i].real
                upper[1, tile(t, i, height), :] = values[i].imag
            return 0

        lax.fori_loop(0, height // ROWS, over_x, 0)

        block = next(n for n in (512, 256, 128, 64, 32, 16, 8) if edge * height % n == 0)

        def screen(c, _):
            at = pl.ds(pl.multiple_of(c * block, block), block)
            real, imag = split_dot(upper[0, at, :], upper[1, at, :], ahead_ref)
            factor = screen_ref[at, :]
            real, imag = split_dot(real * factor, imag * factor, behind_ref)
            upper[0, at, :] = real
            upper[1, at, :] = imag
            return 0

        lax.fori_loop(0, edge * height // block, screen, 0)

        def back_x(t, _):
            at = [tile(t, i, height) for i in range(edge)]
            values = dft([Number(upper[0, a, :], upper[1, a, :]) for a in at], 1)
            for i in range(edge):
                upper[0, at[i], :] = values[i].real
                upper[1, at[i], :] = values[i].imag
            return 0

        lax.fori_loop(0, height // ROWS, back_x, 0)

        def back_y(t, _):
            at = [across(t, i, height) for i in range(half)]
            values = [Number(upper[0, a, :], upper[1, a, :]) for a in at]
            values = values + [values[edge - i].conj() for i in range(half, edge)]
            for i, value in enumerate(real_back(values)):
                cube[tile(t, i, edge), :] = value
            return 0

        lax.fori_loop(0, tiles, back_y, 0)

        firsts = [first_ref[slot] for slot, _ in picked]

        def collect(g, _):
            planes = [
                cube[pl.ds(pl.multiple_of((g * period + i) * edge, ROWS), edge), :]
                for i in range(period)
            ]
            for q in range(group_chunks):
                k = g * group_chunks + q
                for side in range(2):
                    value = None
                    for i in range(period):
                        begin = i * edge - q * LANES
                        if begin + edge <= 0 or begin >= LANES:
                            continue
                        shift = (begin - side * HALF) % LANES
                        piece = pltpu.roll(planes[i], shift, 1) if shift else planes[i]
                        value = piece if value is None else jnp.where(lane < begin, value, piece)
                    value = value * weights[side]
                    forward = value * moved[side, k]
                    dense[side, k, middle, :] = value * near[side, :, columns(k)]
                    for t in range(tiles):
                        at = pl.ds(t * (ROWS * chunks) + k, ROWS, stride=chunks)
                        act[firsts[side], at, :] += forward[t * ROWS : (t + 1) * ROWS]
            return 0

        lax.fori_loop(0, edge // period, collect, 0)

        homes = []
        for side in range(2):
            slot = picked[side][0]
            homes.append(reach_ref[slot] * orb_dev + lax.rem(second_ref[slot], orb_dev))
        returns = [[-d for d in delta] for delta in offsets]

        def send_back(g, _):
            for side in range(2):
                values = shifted(dense.at[side], returns[side], g * stretch, stretch)
                for i, value in enumerate(values):
                    for t in range(tiles):
                        at = pl.ds(t * (ROWS * chunks) + g * stretch + i, ROWS, stride=chunks)
                        back[homes[side], at, :] += value[t * ROWS : (t + 1) * ROWS]
            return 0

        lax.fori_loop(0, chunks // stretch, send_back, 0)
        return 0

    lax.fori_loop(0, lax.div(found + 1, 2), solve_two, 0)

    slab = plane * edge // LANES // groups
    copies = []
    spans = ((orb_dev, 1), (orb_dev + 1, orb_dev - 1), (2 * orb_dev, orb_dev), (0, orb_dev))
    for i, (begin, count) in enumerate(spans):
        copies.append(
            pltpu.make_async_copy(back.at[pl.ds(begin, count)], back_outs[i], out_sem.at[groups + i])
        )
    for k in range(groups):
        source = (member ^ k) * slab
        place = reversed_bits(k, groups)
        copies.append(
            pltpu.make_async_copy(
                act.at[:, pl.ds(pl.multiple_of(source, ROWS), slab), :],
                act_outs[2 * place // groups].at[place % (groups // 2)],
                out_sem.at[k],
            )
        )
    for copy in copies:
        copy.start()
    for copy in copies:
        copy.wait()


def reversed_bits(k, count):
    bits = count.bit_length() - 1
    return sum(((k >> i) & 1) << (bits - 1 - i) for i in range(bits))


def pair_terms(places, pair_count, pair_first, pair_second, pair_reach, anchors, screen, pieces, far):
    orb_dev, edge, plane = pieces[0].shape
    groups = len(pieces)
    frag_size = groups * orb_dev
    fragments = anchors.shape[0]
    slots = pair_first.shape[0]
    chunks = plane // LANES
    rows = edge * chunks
    height = padded_half(edge)
    returns_count = (REACH + 1) * orb_dev
    spots = np.arange(plane, dtype=np.int32).reshape(chunks, LANES)
    spots = jnp.asarray(np.stack([spots // edge, spots % edge]))
    ahead, behind = lane_matrices(edge)
    shape = (edge, orb_dev, groups, fragments, slots)
    smem = pl.BlockSpec(memory_space=pltpu.SMEM)
    hbm = pl.BlockSpec(memory_space=pltpu.HBM)
    f32 = jnp.float32
    tables = [spots, screen, jnp.asarray(ahead), jnp.asarray(behind)]
    found = pl.pallas_call(
        functools.partial(pair_kernel, shape),
        out_shape=[jax.ShapeDtypeStruct((groups // 2, frag_size, rows // groups, LANES), f32)] * 2
        + [
            jax.ShapeDtypeStruct((count, rows, LANES), f32)
            for count in (1, orb_dev - 1, orb_dev, orb_dev)
        ],
        in_specs=[smem] * 6 + [hbm] * (4 + groups + len(far)),
        out_specs=[hbm] * 6,
        scratch_shapes=[
            pltpu.VMEM((frag_size, rows, LANES), f32),
            pltpu.VMEM((returns_count, rows, LANES), f32),
            pltpu.VMEM((2, edge, plane), f32),
            pltpu.VMEM((2, edge, plane), f32),
            pltpu.VMEM((2, chunks, 3 * edge, LANES), f32),
            pltpu.VMEM((2, chunks, edge, LANES), f32),
            pltpu.VMEM((2, chunks, 3 * edge, LANES), f32),
            pltpu.VMEM((plane, LANES), f32),
            pltpu.VMEM((2, height * edge, LANES), f32),
            pltpu.VMEM((2, height * edge, LANES), f32),
            pltpu.SMEM((slots,), jnp.int32),
            pltpu.SemaphoreType.DMA((2, 2)),
            pltpu.SemaphoreType.DMA((groups + 4,)),
            *[pltpu.VMEM(table.shape, table.dtype) for table in tables],
            pltpu.SemaphoreType.DMA((4,)),
        ],
        compiler_params=pltpu.CompilerParams(vmem_limit_bytes=40 << 20),
        name="pair_terms",
    )(
        places, pair_count, pair_first, pair_second, pair_reach, anchors,
        *tables, *pieces, *far,
    )
    return found[:2], found[2:]


def flatten_kernel(shape, places_ref, *refs):
    edge, orb_dev, groups = shape
    pieces, (flat_ref, slab_ref) = refs[:groups], refs[groups:]
    member = places_ref[1]
    chunks = edge * edge // LANES
    slab = slab_ref.shape[1]
    for k in range(groups):
        for o in range(orb_dev):
            def move(j, _):
                value = pieces[k][o, :, pl.ds(pl.multiple_of(j * LANES, LANES), LANES)]
                for t in range(edge // ROWS):
                    at = pl.ds(t * (ROWS * chunks) + j, ROWS, stride=chunks)
                    flat_ref[k * orb_dev + o, at, :] = value[t * ROWS : (t + 1) * ROWS]
                return 0

            lax.fori_loop(0, chunks, move, 0)
    slab_ref[...] = flat_ref[:, pl.ds(pl.multiple_of(member * slab, ROWS), slab), :]


def flatten_terms(places, pieces):
    orb_dev, edge, plane = pieces[0].shape
    groups = len(pieces)
    rows = edge * plane // LANES
    frag_size = groups * orb_dev
    smem = pl.BlockSpec(memory_space=pltpu.SMEM)
    vmem = pl.BlockSpec(memory_space=pltpu.VMEM)
    return pl.pallas_call(
        functools.partial(flatten_kernel, (edge, orb_dev, groups)),
        out_shape=(
            jax.ShapeDtypeStruct((frag_size, rows, LANES), jnp.float32),
            jax.ShapeDtypeStruct((frag_size, rows // groups, LANES), jnp.float32),
        ),
        in_specs=[smem] + [vmem] * groups,
        out_specs=(vmem, vmem),
        compiler_params=pltpu.CompilerParams(vmem_limit_bytes=24 << 20),
        name="flatten_terms",
    )(places, *pieces)


def home_kernel(shape, places_ref, flat_ref, phi_ref, kept_ref, *refs):
    edge, orb_dev, groups, parts = shape
    arrived, refs = refs[:parts], refs[parts:]
    (own_ref, twin_ref, relay_ref, one_ref, two_ref), refs = refs[:5], refs[5:]
    act_ref, outs, total = refs[0], refs[1 : 1 + groups], refs[1 + groups]
    fragment, member = places_ref[0], places_ref[1]
    odd = lax.rem(fragment, 2) == 1
    frag_size = orb_dev * groups
    slab = act_ref.shape[1]
    rows = flat_ref.shape[1]
    cut = frag_size // parts
    for i in range(parts):
        span = slice(i * cut, (i + 1) * cut)
        act_ref[span] = kept_ref[0, span] + arrived[i][0]

    @pl.when(odd)
    def _():
        total[0] = own_ref[0] + two_ref[0] + twin_ref[0]

    @pl.when(jnp.logical_not(odd))
    def _():
        total[0] = own_ref[0] + two_ref[0] + relay_ref[0]

    for o in range(1, orb_dev):
        total[o] = own_ref[o] + two_ref[o] + one_ref[o - 1]

    row = lax.broadcasted_iota(jnp.int32, (frag_size, LANES), 0)
    lane = lax.broadcasted_iota(jnp.int32, (frag_size, LANES), 1)

    def products(lefts, rights, length, step):
        def add(i, sums):
            at = pl.ds(pl.multiple_of(i * step, ROWS), step)
            right = [ref[index, at, :].reshape(step // ROWS, ROWS, LANES) for ref, index in rights]
            out = []
            for n, (ref, index) in enumerate(lefts):
                left = ref[index, at, :].reshape(step // ROWS, ROWS, LANES)
                for m in range(len(rights)):
                    out.append(sums[n * len(rights) + m] + jnp.sum(left * right[m], axis=0))
            return tuple(out)

        zero = jnp.zeros((ROWS, LANES), jnp.float32)
        return lax.fori_loop(0, length // step, add, (zero,) * (len(lefts) * len(rights)))

    result = jnp.zeros((frag_size, LANES), jnp.float32)
    scale = 1.0 / float(edge**3)
    step = next(n for n in (72, 24, 8) if slab % n == 0)
    for half in range(0, frag_size, 4):
        bs = range(half, min(half + 4, frag_size))
        sums = products(
            [(phi_ref, a) for a in range(frag_size)], [(act_ref, b) for b in bs], slab, step
        )
        for a in range(frag_size):
            place = (member ^ (a // orb_dev)) * orb_dev + a % orb_dev
            for i, b in enumerate(bs):
                value = jnp.sum(sums[a * len(bs) + i], keepdims=True)
                result = jnp.where((row == place) & (lane == b), value, result)
    sums = products(
        [(flat_ref, a) for a in range(frag_size)], [(total, b) for b in range(orb_dev)], rows, step
    )
    for a in range(frag_size):
        place = (member ^ (a // orb_dev)) * orb_dev + a % orb_dev
        for b in range(orb_dev):
            value = jnp.sum(sums[a * orb_dev + b], keepdims=True)
            at = (row == place) & (lane == member * orb_dev + b)
            result = jnp.where(at, result + value, result)

    for k in range(groups):
        begin = pl.multiple_of((member ^ k) * slab, ROWS)
        for o in range(orb_dev):
            outs[k][o * slab : (o + 1) * slab, :] = total[o, pl.ds(begin, slab), :]
        outs[k][orb_dev * slab :, :] = result * scale


def home_terms(places, edge, flat, phi, kept, arrived, own, twin, relay, one, two):
    frag_size, slab = phi.shape[:2]
    orb_dev, rows = own.shape[:2]
    groups = frag_size // orb_dev
    smem = pl.BlockSpec(memory_space=pltpu.SMEM)
    vmem = pl.BlockSpec(memory_space=pltpu.VMEM)
    f32 = jnp.float32
    found = pl.pallas_call(
        functools.partial(home_kernel, (edge, orb_dev, groups, len(arrived))),
        out_shape=[jax.ShapeDtypeStruct((frag_size, slab, LANES), f32)]
        + [jax.ShapeDtypeStruct((orb_dev * slab + frag_size, LANES), f32)] * groups,
        in_specs=[smem] + [vmem] * (8 + len(arrived)),
        out_specs=[vmem] * (1 + groups),
        scratch_shapes=[pltpu.VMEM((orb_dev, rows, LANES), f32)],
        compiler_params=pltpu.CompilerParams(vmem_limit_bytes=32 << 20),
        name="home_terms",
    )(places, flat, phi, kept, *arrived, own, twin, relay, one, two)
    return found[0], found[1:]


def gradient_kernel(shape, places_ref, act_ref, phi_ref, *refs):
    edge, orb_dev, groups = shape
    parcels, (out_ref, lagrange_ref, weights, hold) = refs[:groups], refs[groups:]
    member = places_ref[1]
    frag_size = orb_dev * groups
    chunks = edge * edge // LANES
    slab_rows = edge // groups
    slab = slab_rows * chunks
    sums = [parcel[orb_dev * slab :, :] for parcel in parcels]
    while len(sums) > 1:
        sums = [sums[i] + sums[i + 1] for i in range(0, len(sums), 2)]
    square = jnp.concatenate([sums[0], jnp.zeros((LANES - frag_size, LANES), jnp.float32)], axis=0)
    lagrange = 0.5 * (square + square.T)[:frag_size, :]
    lagrange_ref[...] = lagrange[:, :frag_size]
    weights[...] = lagrange

    for k in range(groups):
        for o in range(orb_dev):
            a = (member ^ k) * orb_dev + o
            value = act_ref[a] + parcels[k][o * slab : (o + 1) * slab, :]
            lane = lax.broadcasted_iota(jnp.int32, (1, LANES), 1)
            for q in range(groups):
                for p in range(orb_dev):
                    line = weights[pl.ds((member ^ q) * orb_dev + p, 1), :]
                    factor = jnp.sum(jnp.where(lane == a, line, 0.0), axis=1, keepdims=True)
                    value = value - factor * phi_ref[q * orb_dev + p]
            hold[pl.ds(pl.multiple_of(a * slab, ROWS), slab), :] = value
    for x in range(slab_rows):
        for j in range(chunks):
            value = hold[pl.ds(x * chunks + j, frag_size, stride=slab), :]
            out_ref[x, :, j * LANES : (j + 1) * LANES] = value


def gradient_terms(places, edge, act, phi, parcels):
    groups = len(parcels)
    frag_size, slab = act.shape[:2]
    smem = pl.BlockSpec(memory_space=pltpu.SMEM)
    vmem = pl.BlockSpec(memory_space=pltpu.VMEM)
    f32 = jnp.float32
    gradient, lagrange = pl.pallas_call(
        functools.partial(gradient_kernel, (edge, frag_size // groups, groups)),
        out_shape=(
            jax.ShapeDtypeStruct((edge // groups, frag_size, edge * edge), f32),
            jax.ShapeDtypeStruct((frag_size, frag_size), f32),
        ),
        in_specs=[smem] + [vmem] * (2 + groups),
        out_specs=(vmem, vmem),
        scratch_shapes=[
            pltpu.VMEM((frag_size, LANES), f32),
            pltpu.VMEM((frag_size * slab, LANES), f32),
        ],
        compiler_params=pltpu.CompilerParams(vmem_limit_bytes=24 << 20),
        name="gradient_terms",
    )(places, act, phi, *parcels)
    return gradient.transpose(1, 0, 2), lagrange


def to_fragment(block, distance, senders=None):
    devices = lax.axis_size("orb")
    senders = range(devices) if senders is None else range(senders, devices, 2)
    return lax.ppermute(block, "orb", [(i, (i + distance) % devices) for i in senders])


def with_twin(block):
    return lax.ppermute(block, "orb", [(i, i ^ 1) for i in range(lax.axis_size("orb"))])


def with_member(block, bit):
    return lax.ppermute(block, "grp", [(i, i ^ bit) for i in range(lax.axis_size("grp"))])


def shards(orbitals, kernel, anchors, pair_count, pair_first, pair_second, pair_reach):
    groups = lax.axis_size("grp")
    orb_dev, edge, plane = orbitals.shape
    frag_size = groups * orb_dev
    places = jnp.stack([lax.axis_index("orb"), lax.axis_index("grp")]).astype(jnp.int32)
    screen = screen_terms(kernel)

    two = to_fragment(orbitals, -2)
    twin = with_twin(orbitals[:1])
    one = to_fragment(orbitals[1:], -1)
    relay = to_fragment(twin, -2, 1)
    pieces = {0: orbitals}
    bit = groups // 2
    while bit:
        for k in list(pieces):
            pieces[k ^ bit] = with_member(pieces[k], bit)
        bit //= 2
    pieces = [pieces[k] for k in range(groups)]

    (kept, sent), (back_first, back_rest, back_two, own) = pair_terms(
        places, pair_count, pair_first, pair_second, pair_reach, anchors, screen,
        pieces, [twin, relay, one, two],
    )

    two = to_fragment(back_two, 2)
    twin = with_twin(back_first)
    one = to_fragment(back_rest, 1)
    relay = to_fragment(twin, 2, 0)

    bit = 1
    arrived = [with_member(sent, bit)]
    while 2 * bit < groups:
        kept = kept + jnp.concatenate(arrived, axis=1)
        half = kept.shape[0] // 2
        cut = frag_size // orb_dev
        bit *= 2
        arrived = [
            with_member(kept[half:, i : i + cut], bit) for i in range(0, frag_size, cut)
        ]
        kept = kept[:half]

    flat, phi = flatten_terms(places, pieces)
    act, parcels = home_terms(places, edge, flat, phi, kept, arrived, own, twin, relay, one, two)
    received = []
    for k in range(groups):
        parcel, bit = parcels[k], groups // 2
        while bit:
            if k & bit:
                parcel = with_member(parcel, bit)
            bit //= 2
        received.append(parcel)
    gradient, lagrange = gradient_terms(places, edge, act, phi, received)
    return (gradient, lagrange[None])


def solution(mesh):
    placed = (P(("orb", "grp"), None, None), P(), P(), P("orb"), P("orb"), P("orb"), P("orb"))
    return jax.shard_map(
        shards,
        mesh=mesh,
        in_specs=placed,
        out_specs=(P("orb", "grp", None), P("orb", None, None)),
        check_vma=False,
    )
```

profile of v0, /device:TPU:0, one launch (start us, length us, event | category | flops | bytes accessed | tf_op | source)
XLA Modules:
  0.0 118.9 jit_solution(7624230408866010960)
XLA Ops:
  0.7 3.0 %collective-permute-start.1 = (f32[2,48,2304]{2,1,0:T(8,128)}, f32[2,48,2304]{2,1,0:T(8,128)S(1)}, u32[]{:S(2)}, u32[]{:S(2)}) collective-permute-start(f32[2,48,2304]{2,1,0:T(8,128)} %refs_4_.1), channel_id=1, source_target_pairs={{0,2},{1,3},{2,0},{3,1},{4,6},{5,7},{6,4},{7,5},{8,10},{9,11},{10,... | collective-permute-start | bytes 2654216 | tf_op jit(solution)/shard_map/ppermute | solution.py:878
  3.7 2.0 %fusion.1 = (f32[1,48,2304]{2,1,0:T(8,128)}, f32[1,48,2304]{2,1,0:T(8,128)S(1)}) fusion(f32[2,48,2304]{2,1,0:T(8,128)} %refs_4_.1), kind=kLoop, calls=%fused_computation.2 | loop fusion | bytes 1769472 | tf_op jit(solution)/shard_map/slice | solution.py:890
  5.7 1.5 %collective-permute-start.3 = (f32[1,48,2304]{2,1,0:T(8,128)S(1)}, f32[1,48,2304]{2,1,0:T(8,128)}, u32[]{:S(2)}, u32[]{:S(2)}) collective-permute-start(f32[1,48,2304]{2,1,0:T(8,128)S(1)} %get-tuple-element.35), channel_id=1, source_target_pairs={{0,4},{4,0},{8,12},{12,8},{16,20},{20,16},{24,28},{28,24},{1,5},{5... | collective-permute-start | bytes 1327112 | tf_op jit(solution)/shard_map/ppermute | solution.py:874
  7.2 3.6 %collective-permute-start.6 = (f32[2,48,2304]{2,1,0:T(8,128)S(1)}, f32[2,48,2304]{2,1,0:T(8,128)}, u32[]{:S(2)}, u32[]{:S(2)}) collective-permute-start(f32[2,48,2304]{2,1,0:T(8,128)S(1)} %copy-done), channel_id=1, source_target_pairs={{0,24},{4,28},{8,0},{12,4},{16,8},{20,12},{24,16},{28,20},{1,25},{... | collective-permute-start | bytes 2654216 | tf_op jit(solution)/shard_map/ppermute | solution.py:870
  10.8 12.8 %collective-permute-done.1.refs_2_.refs_6_ = f32[2,48,2304]{2,1,0:T(8,128)S(1)} collective-permute-done((f32[2,48,2304]{2,1,0:T(8,128)}, f32[2,48,2304]{2,1,0:T(8,128)S(1)}, u32[]{:S(2)}, u32[]{:S(2)}) %collective-permute-start.1) | collective-permute-done | bytes 884768 | tf_op jit(solution)/shard_map/ppermute | solution.py:878
  23.6 4.8 %collective-permute-start.5 = (f32[1,48,2304]{2,1,0:T(8,128)}, f32[1,48,2304]{2,1,0:T(8,128)}, u32[]{:S(2)}, u32[]{:S(2)}) collective-permute-start(f32[1,48,2304]{2,1,0:T(8,128)} %get-tuple-element.34), channel_id=1, source_target_pairs={{0,28},{4,0},{8,4},{12,8},{16,12},{20,16},{24,20},{28,24},{1,29},{... | collective-permute-start | bytes 1327112 | tf_op jit(solution)/shard_map/ppermute | solution.py:870
  28.3 1.4 %collective-permute-start.4 = (f32[1,48,2304]{2,1,0:T(8,128)}, f32[1,48,2304]{2,1,0:T(8,128)}, u32[]{:S(2)}, u32[]{:S(2)}) collective-permute-start(f32[1,48,2304]{2,1,0:T(8,128)} %collective-permute-done.3.refs_8_), channel_id=1, source_target_pairs={{4,28},{12,4},{20,12},{28,20},{5,29},{13,5},{21,13},{29,21},{6,30}... | collective-permute-start | bytes 1327112 | tf_op jit(solution)/shard_map/ppermute | solution.py:870
  29.8 0.8 copy.14.anchors_ref
  31.2 1.0 copy-done.1
  32.2 0.8 copy-done.4
  33.0 0.7 copy-done.6
  33.8 2.5 %screen_terms.1.refs_1_ = f32[1536,128]{1,0:T(8,128)S(1)} custom-call(f32[48,2304]{1,0:T(8,128)S(1)} %copy-done.1, f32[48,48]{1,0:T(8,128)S(1)} %copy-done.6, f32[128,128]{1,0:T(8,128)S(1)} %copy-done.4), custom_call_target="tpu_custom_call" | custom-call | tf_op jit(solution)/shard_map/screen_terms/pallas_call | solution.py:290
  36.4 3.6 %collective-permute-done.5.refs_10_ = f32[1,48,2304]{2,1,0:T(8,128)} collective-permute-done((f32[1,48,2304]{2,1,0:T(8,128)}, f32[1,48,2304]{2,1,0:T(8,128)}, u32[]{:S(2)}, u32[]{:S(2)}) %collective-permute-start.5) | collective-permute-done | bytes 442400 | tf_op jit(solution)/shard_map/ppermute | solution.py:870
  40.0 0.9 copy-done.2
  40.9 0.9 copy-done.3
  41.9 0.7 copy-done.5
  42.6 12.6 %pair_terms.1 = (f32[2,8,216,128]{3,2,1,0:T(8,128)S(1)}, f32[2,8,216,128]{3,2,1,0:T(8,128)S(1)}, f32[1,864,128]{2,1,0:T(8,128)S(1)}, f32[1,864,128]{2,1,0:T(8,12...) custom-call(s32[2]{0:T(128)S(1)} %pad_add_fusion.places_ref, s32[1]{0:T(128)S(6)} %copy.15.count_ref, ...), custom_call_target="tpu_custom_call" | custom-call | tf_op jit(solution)/shard_map/pair_terms/pallas_call | solution.py:643
  55.4 1.9 %collective-permute-start.10 = (f32[1,864,128]{2,1,0:T(8,128)S(1)}, f32[1,864,128]{2,1,0:T(8,128)S(1)}, u32[]{:S(2)}, u32[]{:S(2)}) collective-permute-start(f32[1,864,128]{2,1,0:T(8,128)S(1)} %get-tuple-element.22), channel_id=1, source_target_pairs={{0,4},{4,0},{8,12},{12,8},{16,20},{20,16},{24,28},{28,24},{1,5},{5... | collective-permute-start | bytes 1327112 | tf_op jit(solution)/shard_map/ppermute | solution.py:874
  57.2 0.4 collective-permute-start.13
  57.7 10.3 %collective-permute-done.10.refs_3_ = f32[1,864,128]{2,1,0:T(8,128)S(1)} collective-permute-done((f32[1,864,128]{2,1,0:T(8,128)S(1)}, f32[1,864,128]{2,1,0:T(8,128)S(1)}, u32[]{:S(2)}, u32[]{:S(2)}) %collective-permute-start.10) | collective-permute-done | bytes 442400 | tf_op jit(solution)/shard_map/ppermute | solution.py:874
  68.0 2.3 %collective-permute-start.11 = (f32[1,864,128]{2,1,0:T(8,128)S(1)}, f32[1,864,128]{2,1,0:T(8,128)S(1)}, u32[]{:S(2)}, u32[]{:S(2)}) collective-permute-start(f32[1,864,128]{2,1,0:T(8,128)S(1)} %collective-permute-done.10.refs_3_), channel_id=1, source_target_pairs={{0,8},{8,16},{16,24},{24,0},{1,9},{9,17},{17,25},{25,1},{2,10},{10... | collective-permute-start | bytes 1327112 | tf_op jit(solution)/shard_map/ppermute | solution.py:870
  70.6 11.9 %collective-permute-start.8 = (f32[1,4,216,128]{3,2,1,0:T(8,128)S(1)}, f32[1,4,216,128]{3,2,1,0:T(8,128)S(1)}, u32[]{:S(2)}, u32[]{:S(2)}) collective-permute-start(f32[1,4,216,128]{3,2,1,0:T(8,128)S(1)} %get-tuple-element.33), channel_id=1, source_target_pairs={{0,2},{1,3},{2,0},{3,1},{4,6},{5,7},{6,4},{7,5},{8,10},{9,11},{10,... | collective-permute-start | bytes 1327112 | tf_op jit(solution)/shard_map/ppermute | solution.py:878
  82.6 1.5 %flatten_terms.1 = (f32[8,864,128]{2,1,0:T(8,128)S(1)}, f32[8,216,128]{2,1,0:T(8,128)S(1)}) custom-call(s32[2]{0:T(128)S(1)} %pad_add_fusion.places_ref, f32[2,48,2304]{2,1,0:T(8,128)S(1)} %copy-done, f32[2,48,2304]{2,1,0:T(8,128)S(1)} %collective-permute-done.refs_1_.refs_5_, f32[2,48,2304]{2,1,0:T(8,128)S(1)} %collective-permute-done.1.refs_2_.refs_6_, ...), custom_call_target="tpu_custom_call" | custom-call | tf_op jit(solution)/shard_map/flatten_terms/pallas_call | solution.py:704
  84.2 5.8 %collective-permute-done.12.refs_5_ = f32[1,864,128]{2,1,0:T(8,128)S(1)} collective-permute-done((f32[1,864,128]{2,1,0:T(8,128)S(1)}, f32[1,864,128]{2,1,0:T(8,128)S(1)}, u32[]{:S(2)}, u32[]{:S(2)}) %collective-permute-start.12) | collective-permute-done | bytes 442400 | tf_op jit(solution)/shard_map/ppermute | solution.py:870
  90.0 0.3 collective-permute-done.11.refs_4_
  90.2 3.2 %collective-permute-done.8.refs_0_ = f32[1,4,216,128]{3,2,1,0:T(8,128)S(1)} collective-permute-done((f32[1,4,216,128]{3,2,1,0:T(8,128)S(1)}, f32[1,4,216,128]{3,2,1,0:T(8,128)S(1)}, u32[]{:S(2)}, u32[]{:S(2)}) %collective-permute-start.8) | collective-permute-done | bytes 442400 | tf_op jit(solution)/shard_map/ppermute | solution.py:878
  93.5 8.7 %collective-permute-done.9.refs_1_ = f32[1,4,216,128]{3,2,1,0:T(8,128)S(1)} collective-permute-done((f32[1,4,216,128]{3,2,1,0:T(8,128)S(1)}, f32[1,4,216,128]{3,2,1,0:T(8,128)S(1)}, u32[]{:S(2)}, u32[]{:S(2)}) %collective-permute-start.9) | collective-permute-done | bytes 442400 | tf_op jit(solution)/shard_map/ppermute | solution.py:878
  102.2 2.4 %home_terms.1 = (f32[8,216,128]{2,1,0:T(8,128)S(1)}, f32[440,128]{1,0:T(8,128)S(1)}, f32[440,128]{1,0:T(8,128)S(1)}, f32[440,128]{1,0:T(8,128)S(1)}, f32[440,128]{1,0:T(8,128)S(1)}) custom-call(s32[2]{0:T(128)S(1)} %pad_add_fusion.places_ref, f32[8,864,128]{2,1,0:T(8,128)S(1)} %get-tuple-element.17.flat_ref, f32[8,216,128]{2,1,0:T(8,128)S(1)} %get-tuple-element.18.phi_ref, ...), custom_call_target="tpu_custom_call" | custom-call | tf_op jit(solution)/shard_map/home_terms/pallas_call | solution.py:797
  104.6 1.8 %collective-permute-start.16 = (f32[440,128]{1,0:T(8,128)S(1)}, f32[440,128]{1,0:T(8,128)S(1)}, u32[]{:S(2)}, u32[]{:S(2)}) collective-permute-start(f32[440,128]{1,0:T(8,128)S(1)} %get-tuple-element.29), channel_id=1, source_target_pairs={{0,2},{1,3},{2,0},{3,1},{4,6},{5,7},{6,4},{7,5},{8,10},{9,11},{10,... | collective-permute-start | bytes 675848 | tf_op jit(solution)/shard_map/ppermute | solution.py:878
  106.6 6.4 %collective-permute-done.16 = f32[440,128]{1,0:T(8,128)S(1)} collective-permute-done((f32[440,128]{1,0:T(8,128)S(1)}, f32[440,128]{1,0:T(8,128)S(1)}, u32[]{:S(2)}, u32[]{:S(2)}) %collective-permute-start.16) | collective-permute-done | bytes 225312 | tf_op jit(solution)/shard_map/ppermute | solution.py:878
  113.1 3.1 %collective-permute-done.15.refs_2_ = f32[440,128]{1,0:T(8,128)S(1)} collective-permute-done((f32[440,128]{1,0:T(8,128)S(1)}, f32[440,128]{1,0:T(8,128)S(1)}, u32[]{:S(2)}, u32[]{:S(2)}) %collective-permute-start.15) | collective-permute-done | bytes 225312 | tf_op jit(solution)/shard_map/ppermute | solution.py:878
  116.2 2.8 %gradient_terms.1 = (f32[12,8,2304]{2,1,0:T(8,128)}, f32[8,8]{1,0:T(8,128)}) custom-call(s32[2]{0:T(128)S(1)} %pad_add_fusion.places_ref, f32[8,216,128]{2,1,0:T(8,128)S(1)} %get-tuple-element.25.act_ref, f32[8,216,128]{2,1,0:T(8,128)S(1)} %get-tuple-element.18.phi_ref, f32[440,128]{1,0:T(8,128)S(1)} %get-tuple-element.26.refs_0_, ...), custom_call_target="tpu_custom_call" | custom-call | tf_op jit(solution)/shard_map/gradient_terms/pallas_call | solution.py:849
  (35 shorter events, 1.0 us)
Async XLA Ops:
  0.6 6.5 %copy-start = (f32[2,48,2304]{2,1,0:T(8,128)S(1)}, f32[2,48,2304]{2,1,0:T(8,128)}, u32[]{:S(2)}) copy-start(f32[2,48,2304]{2,1,0:T(8,128)} %refs_4_.1) | copy-start | bytes 2654212
  0.6 39.3 %copy-start.7 = (s32[8]{0:T(128)S(1)}, s32[8]{0:T(128)}, u32[]{:S(2)}) copy-start(s32[8]{0:T(128)} %first_ref.1) | copy-start | bytes 100
  0.7 39.3 %copy-start.8 = (s32[8]{0:T(128)S(1)}, s32[8]{0:T(128)}, u32[]{:S(2)}) copy-start(s32[8]{0:T(128)} %second_ref.1) | copy-start | bytes 100
  0.7 39.3 %copy-start.9 = (s32[8]{0:T(128)S(1)}, s32[8]{0:T(128)}, u32[]{:S(2)}) copy-start(s32[8]{0:T(128)} %reach_ref.1) | copy-start | bytes 100
  0.7 22.9 %collective-permute-start.1 = (f32[2,48,2304]{2,1,0:T(8,128)}, f32[2,48,2304]{2,1,0:T(8,128)S(1)}, u32[]{:S(2)}, u32[]{:S(2)}) collective-permute-start(f32[2,48,2304]{2,1,0:T(8,128)} %refs_4_.1), channel_id=1, source_target_pairs={{0,2},{1,3},{2,0},{3,1},{4,6},{5,7},{6,4},{7,5},{8,10},{9,11},{10,... | collective-permute-start | bytes 2654216 | tf_op jit(solution)/shard_map/ppermute | solution.py:878
  5.7 22.6 %collective-permute-start.3 = (f32[1,48,2304]{2,1,0:T(8,128)S(1)}, f32[1,48,2304]{2,1,0:T(8,128)}, u32[]{:S(2)}, u32[]{:S(2)}) collective-permute-start(f32[1,48,2304]{2,1,0:T(8,128)S(1)} %get-tuple-element.35), channel_id=1, source_target_pairs={{0,4},{4,0},{8,12},{12,8},{16,20},{20,16},{24,28},{28,24},{1,5},{5... | collective-permute-start | bytes 1327112 | tf_op jit(solution)/shard_map/ppermute | solution.py:874
  7.2 32.8 %collective-permute-start = (f32[2,48,2304]{2,1,0:T(8,128)S(1)}, f32[2,48,2304]{2,1,0:T(8,128)S(1)}, u32[]{:S(2)}, u32[]{:S(2)}) collective-permute-start(f32[2,48,2304]{2,1,0:T(8,128)S(1)} %copy-done), channel_id=1, source_target_pairs={{0,1},{1,0},{2,3},{3,2},{4,5},{5,4},{6,7},{7,6},{8,9},{9,8},{10,11... | collective-permute-start | bytes 2654216 | tf_op jit(solution)/shard_map/ppermute | solution.py:878
  7.2 32.8 %collective-permute-start.6 = (f32[2,48,2304]{2,1,0:T(8,128)S(1)}, f32[2,48,2304]{2,1,0:T(8,128)}, u32[]{:S(2)}, u32[]{:S(2)}) collective-permute-start(f32[2,48,2304]{2,1,0:T(8,128)S(1)} %copy-done), channel_id=1, source_target_pairs={{0,24},{4,28},{8,0},{12,4},{16,8},{20,12},{24,16},{28,20},{1,25},{... | collective-permute-start | bytes 2654216 | tf_op jit(solution)/shard_map/ppermute | solution.py:870
  23.6 16.4 %collective-permute-start.2 = (f32[2,48,2304]{2,1,0:T(8,128)S(1)}, f32[2,48,2304]{2,1,0:T(8,128)S(1)}, u32[]{:S(2)}, u32[]{:S(2)}) collective-permute-start(f32[2,48,2304]{2,1,0:T(8,128)S(1)} %collective-permute-done.1.refs_2_.refs_6_), channel_id=1, source_target_pairs={{0,1},{1,0},{2,3},{3,2},{4,5},{5,4},{6,7},{7,6},{8,9},{9,8},{10,11... | collective-permute-start | bytes 2654216 | tf_op jit(solution)/shard_map/ppermute | solution.py:878
  23.6 16.4 %collective-permute-start.5 = (f32[1,48,2304]{2,1,0:T(8,128)}, f32[1,48,2304]{2,1,0:T(8,128)}, u32[]{:S(2)}, u32[]{:S(2)}) collective-permute-start(f32[1,48,2304]{2,1,0:T(8,128)} %get-tuple-element.34), channel_id=1, source_target_pairs={{0,28},{4,0},{8,4},{12,8},{16,12},{20,16},{24,20},{28,24},{1,29},{... | collective-permute-start | bytes 1327112 | tf_op jit(solution)/shard_map/ppermute | solution.py:870
  28.3 11.6 %collective-permute-start.4 = (f32[1,48,2304]{2,1,0:T(8,128)}, f32[1,48,2304]{2,1,0:T(8,128)}, u32[]{:S(2)}, u32[]{:S(2)}) collective-permute-start(f32[1,48,2304]{2,1,0:T(8,128)} %collective-permute-done.3.refs_8_), channel_id=1, source_target_pairs={{4,28},{12,4},{20,12},{28,20},{5,29},{13,5},{21,13},{29,21},{6,30}... | collective-permute-start | bytes 1327112 | tf_op jit(solution)/shard_map/ppermute | solution.py:870
  31.2 1.0 copy-start.1
  32.2 0.8 copy-start.4
  33.0 0.7 copy-start.6
  40.0 1.0 copy-start.2
  40.9 0.9 copy-start.3
  41.9 0.7 copy-start.5
  55.3 15.0 %collective-permute-start.7 = (f32[2,8,216,128]{3,2,1,0:T(8,128)S(1)}, f32[2,8,216,128]{3,2,1,0:T(8,128)S(1)}, u32[]{:S(2)}, u32[]{:S(2)}) collective-permute-start(f32[2,8,216,128]{3,2,1,0:T(8,128)S(1)} %get-tuple-element.20), channel_id=1, source_target_pairs={{0,1},{1,0},{2,3},{3,2},{4,5},{5,4},{6,7},{7,6},{8,9},{9,8},{10,11... | collective-permute-start | bytes 5308424 | tf_op jit(solution)/shard_map/ppermute | solution.py:878
  55.4 12.6 %collective-permute-start.10 = (f32[1,864,128]{2,1,0:T(8,128)S(1)}, f32[1,864,128]{2,1,0:T(8,128)S(1)}, u32[]{:S(2)}, u32[]{:S(2)}) collective-permute-start(f32[1,864,128]{2,1,0:T(8,128)S(1)} %get-tuple-element.22), channel_id=1, source_target_pairs={{0,4},{4,0},{8,12},{12,8},{16,20},{20,16},{24,28},{28,24},{1,5},{5... | collective-permute-start | bytes 1327112 | tf_op jit(solution)/shard_map/ppermute | solution.py:874
  57.2 33.0 %collective-permute-start.13 = (f32[2,864,128]{2,1,0:T(8,128)S(1)}, f32[2,864,128]{2,1,0:T(8,128)S(1)}, u32[]{:S(2)}, u32[]{:S(2)}) collective-permute-start(f32[2,864,128]{2,1,0:T(8,128)S(1)} %get-tuple-element.24), channel_id=1, source_target_pairs={{0,8},{4,12},{8,16},{12,20},{16,24},{20,28},{24,0},{28,4},{1,9},{5... | collective-permute-start | bytes 2654216 | tf_op jit(solution)/shard_map/ppermute | solution.py:870
  57.6 32.3 %collective-permute-start.12 = (f32[1,864,128]{2,1,0:T(8,128)S(1)}, f32[1,864,128]{2,1,0:T(8,128)S(1)}, u32[]{:S(2)}, u32[]{:S(2)}) collective-permute-start(f32[1,864,128]{2,1,0:T(8,128)S(1)} %get-tuple-element.23), channel_id=1, source_target_pairs={{0,4},{4,8},{8,12},{12,16},{16,20},{20,24},{24,28},{28,0},{1,5},{5... | collective-permute-start | bytes 1327112 | tf_op jit(solution)/shard_map/ppermute | solution.py:870
  68.0 22.2 %collective-permute-start.11 = (f32[1,864,128]{2,1,0:T(8,128)S(1)}, f32[1,864,128]{2,1,0:T(8,128)S(1)}, u32[]{:S(2)}, u32[]{:S(2)}) collective-permute-start(f32[1,864,128]{2,1,0:T(8,128)S(1)} %collective-permute-done.10.refs_3_), channel_id=1, source_target_pairs={{0,8},{8,16},{16,24},{24,0},{1,9},{9,17},{17,25},{25,1},{2,10},{10... | collective-permute-start | bytes 1327112 | tf_op jit(solution)/shard_map/ppermute | solution.py:870
  70.6 22.9 %collective-permute-start.8 = (f32[1,4,216,128]{3,2,1,0:T(8,128)S(1)}, f32[1,4,216,128]{3,2,1,0:T(8,128)S(1)}, u32[]{:S(2)}, u32[]{:S(2)}) collective-permute-start(f32[1,4,216,128]{3,2,1,0:T(8,128)S(1)} %get-tuple-element.33), channel_id=1, source_target_pairs={{0,2},{1,3},{2,0},{3,1},{4,6},{5,7},{6,4},{7,5},{8,10},{9,11},{10,... | collective-permute-start | bytes 1327112 | tf_op jit(solution)/shard_map/ppermute | solution.py:878
  82.5 19.7 %collective-permute-start.9 = (f32[1,4,216,128]{3,2,1,0:T(8,128)S(1)}, f32[1,4,216,128]{3,2,1,0:T(8,128)S(1)}, u32[]{:S(2)}, u32[]{:S(2)}) collective-permute-start(f32[1,4,216,128]{3,2,1,0:T(8,128)S(1)} %get-tuple-element.32), channel_id=1, source_target_pairs={{0,2},{1,3},{2,0},{3,1},{4,6},{5,7},{6,4},{7,5},{8,10},{9,11},{10,... | collective-permute-start | bytes 1327112 | tf_op jit(solution)/shard_map/ppermute | solution.py:878
  104.6 8.5 %collective-permute-start.16 = (f32[440,128]{1,0:T(8,128)S(1)}, f32[440,128]{1,0:T(8,128)S(1)}, u32[]{:S(2)}, u32[]{:S(2)}) collective-permute-start(f32[440,128]{1,0:T(8,128)S(1)} %get-tuple-element.29), channel_id=1, source_target_pairs={{0,2},{1,3},{2,0},{3,1},{4,6},{5,7},{6,4},{7,5},{8,10},{9,11},{10,... | collective-permute-start | bytes 675848 | tf_op jit(solution)/shard_map/ppermute | solution.py:878
  106.4 6.7 %collective-permute-start.14 = (f32[440,128]{1,0:T(8,128)S(1)}, f32[440,128]{1,0:T(8,128)S(1)}, u32[]{:S(2)}, u32[]{:S(2)}) collective-permute-start(f32[440,128]{1,0:T(8,128)S(1)} %get-tuple-element.27), channel_id=1, source_target_pairs={{0,1},{1,0},{2,3},{3,2},{4,5},{5,4},{6,7},{7,6},{8,9},{9,8},{10,11... | collective-permute-start | bytes 675848 | tf_op jit(solution)/shard_map/ppermute | solution.py:878
  106.4 9.8 %collective-permute-start.15 = (f32[440,128]{1,0:T(8,128)S(1)}, f32[440,128]{1,0:T(8,128)S(1)}, u32[]{:S(2)}, u32[]{:S(2)}) collective-permute-start(f32[440,128]{1,0:T(8,128)S(1)} %get-tuple-element.28), channel_id=1, source_target_pairs={{0,2},{1,3},{2,0},{3,1},{4,6},{5,7},{6,4},{7,5},{8,10},{9,11},{10,... | collective-permute-start | bytes 675848 | tf_op jit(solution)/shard_map/ppermute | solution.py:878
  113.1 3.1 %collective-permute-start.17 = (f32[440,128]{1,0:T(8,128)S(1)}, f32[440,128]{1,0:T(8,128)S(1)}, u32[]{:S(2)}, u32[]{:S(2)}) collective-permute-start(f32[440,128]{1,0:T(8,128)S(1)} %collective-permute-done.16), channel_id=1, source_target_pairs={{0,1},{1,0},{2,3},{3,2},{4,5},{5,4},{6,7},{7,6},{8,9},{9,8},{10,11... | collective-permute-start | bytes 675848 | tf_op jit(solution)/shard_map/ppermute | solution.py:878
where the time goes:
time: 119 us
  waiting for transfers between devices  54.2 us (46%)
  starting transfers between devices  33.1 us (28%)
  Pallas kernels  21.8 us (18%)
  local copies, waits for them, and re-layouts  8.07 us (7%)
  between operations  1.46 us (1%)
    ppermute x10, waiting for transfers between devices, with_member(): lax.ppermute(block, 'grp', [(i, i ^ bit) for i in range(lax.axis_size('gr...  34.2 us
    ppermute x10, starting transfers between devices, with_member(): lax.ppermute(block, 'grp', [(i, i ^ bit) for i in range(lax.axis_size('gr...  17.2 us
    pallas_call x1, Pallas kernels, pair_terms(): pl.pallas_call(functools.partial(pair_kernel, shape), out_shape=[jax.Shap...  12.6 us
    ppermute x6, starting transfers between devices, to_fragment(): lax.ppermute(block, 'orb', [(i, (i + distance) % devices) for i in senders])  12.5 us
    ppermute x2, waiting for transfers between devices, with_twin(): lax.ppermute(block, 'orb', [(i, i ^ 1) for i in range(lax.axis_size('orb'...  10.3 us
    ppermute x6, waiting for transfers between devices, to_fragment(): lax.ppermute(block, 'orb', [(i, (i + distance) % devices) for i in senders])  9.67 us
    unnamed x21, local copies, waits for them, and re-layouts  5.99 us
    ppermute x2, starting transfers between devices, with_twin(): lax.ppermute(block, 'orb', [(i, i ^ 1) for i in range(lax.axis_size('orb'...  3.38 us
  transfers between devices with their start and end apart: 18, of which 9 were waited for; matrix products, arithmetic and copies ran while one was open for 3% of the time, Pallas kernels for 3%

commit v1 on v0

--- a/solution.py
+++ b/solution.py
@@ -235,7 +235,7 @@
         full = np.pad(full, [(0, 0), (0, 0), (0, HALF - edge)] * 2).reshape(2 * LANES, 2 * LANES)
         high = full.astype(jnp.bfloat16)
         low = (full - high.astype(np.float64)).astype(jnp.bfloat16)
-        found.append(np.stack([high, low]))
+        found.append(np.concatenate([high, high, low]))
     return found
 
 
@@ -243,9 +243,9 @@
     value = jnp.concatenate([real, imag], axis=1)
     high = value.astype(jnp.bfloat16)
     low = (value - high.astype(jnp.float32)).astype(jnp.bfloat16)
-    product = jnp.dot(high, matrix[0], preferred_element_type=jnp.float32)
-    product += jnp.dot(low, matrix[0], preferred_element_type=jnp.float32)
-    product += jnp.dot(high, matrix[1], preferred_element_type=jnp.float32)
+    product = jnp.dot(
+        jnp.concatenate([high, low, high], axis=1), matrix[...], preferred_element_type=jnp.float32
+    )
     return product[:, :LANES], product[:, LANES:]
 
 
@@ -253,7 +253,9 @@
     return -(-(edge // 2 + 1) // ROWS) * ROWS
 
 
-def screen_kernel(edge, kernel_ref, flip_ref, mirror_ref, out_ref, flipped):
+def screen_kernel(edge, numbers_ref, kernel_ref, flip_ref, mirror_ref, out_ref, kept_ref, flipped):
+    for i in range(numbers_ref.shape[0]):
+        kept_ref[i] = numbers_ref[i]
     exact = dict(precision=lax.Precision.HIGHEST, preferred_element_type=jnp.float32)
     flipped[...] = jnp.dot(flip_ref[...], kernel_ref[...], **exact)
     height = padded_half(edge)
@@ -278,7 +280,7 @@
             out_ref[pl.ds(t * ROWS * height + y, ROWS, stride=height), :] = value[t * ROWS : (t + 1) * ROWS]
 
 
-def screen_terms(kernel):
+def screen_terms(numbers, kernel):
     edge, plane = kernel.shape
     index = np.arange(edge)
     flip = np.zeros((edge, edge), np.float32)
@@ -286,26 +288,25 @@
     mirror = np.zeros((LANES, LANES), np.float32)
     mirror[-index % edge, index] = 1.0
     mirror[-index % edge, HALF + index] = 1.0
+    smem = pl.BlockSpec(memory_space=pltpu.SMEM)
     vmem = pl.BlockSpec(memory_space=pltpu.VMEM)
     return pl.pallas_call(
         functools.partial(screen_kernel, edge),
-        out_shape=jax.ShapeDtypeStruct((edge * padded_half(edge), LANES), jnp.float32),
-        in_specs=[vmem] * 3,
-        out_specs=vmem,
+        out_shape=(
+            jax.ShapeDtypeStruct((edge * padded_half(edge), LANES), jnp.float32),
+            jax.ShapeDtypeStruct(numbers.shape, numbers.dtype),
+        ),
+        in_specs=[smem] + [vmem] * 3,
+        out_specs=(vmem, smem),
         scratch_shapes=[pltpu.VMEM((edge, plane), jnp.float32)],
         compiler_params=pltpu.CompilerParams(vmem_limit_bytes=16 << 20),
         name="screen_terms",
-    )(kernel, jnp.asarray(flip), jnp.asarray(mirror))
+    )(numbers, kernel, jnp.asarray(flip), jnp.asarray(mirror))
 
 
 def pair_kernel(
     shape,
-    places_ref,
-    count_ref,
-    first_ref,
-    second_ref,
-    reach_ref,
-    anchors_ref,
+    numbers_ref,
     *refs,
 ):
     edge, orb_dev, groups, fragments, slots = shape
@@ -315,19 +316,30 @@
     half = edge // 2 + 1
     height = padded_half(edge)
     returns_count = (REACH + 1) * orb_dev
-    tables, refs = refs[:4], refs[4:]
+    tables, refs = refs[:3], refs[3:]
     phi_refs, refs = refs[:groups], refs[groups:]
     (twin_ref, relay_ref, one_ref, two_ref), refs = refs[:4], refs[4:]
     act_outs, back_outs, refs = refs[:2], refs[2:6], refs[6:]
     (act, back, near, far, wide, moved, dense, cube, lower, upper, listed, load_sem, out_sem) = refs[:13]
-    spots_ref, screen_ref, ahead_ref, behind_ref = refs[13:17]
-    table_sem = refs[17]
-
-    fragment = places_ref[0]
-    member = places_ref[1]
+    screen_ref, ahead_ref, behind_ref, table_sem = refs[13:]
+
+    fragment, member, live_slots = numbers_ref[0], numbers_ref[1], numbers_ref[2]
+
+    def first_of(slot):
+        return numbers_ref[3 + slot]
+
+    def second_of(slot):
+        return numbers_ref[3 + slots + slot]
+
+    def reach_of(slot):
+        return numbers_ref[3 + 2 * slots + slot]
+
+    def anchor(place, axis):
+        return numbers_ref[3 + 3 * slots + 3 * place + axis]
+
     table_copies = [
         pltpu.make_async_copy(table, hold, table_sem.at[i])
-        for i, (table, hold) in enumerate(zip(tables, refs[13:17]))
+        for i, (table, hold) in enumerate(zip(tables, refs[13:16]))
     ]
     for copy in table_copies:
         copy.start()
@@ -339,7 +351,7 @@
     middle = pl.ds(edge, edge)
 
     def list_slots(slot, found):
-        mine = (slot < count_ref[0]) & (lax.div(second_ref[slot], orb_dev) == member)
+        mine = (slot < live_slots) & (lax.div(second_of(slot), orb_dev) == member)
 
         @pl.when(mine)
         def _():
@@ -360,7 +372,7 @@
     def start_loads(turn):
         for side in range(2):
             slot, _ = slot_of(turn, side)
-            first, second, reach = first_ref[slot], second_ref[slot], reach_ref[slot]
+            first, second, reach = first_of(slot), second_of(slot), reach_of(slot)
             relative = lax.div(first, orb_dev) ^ member
             for k in range(groups):
                 @pl.when(relative == k)
@@ -405,8 +417,21 @@
         copy.wait()
 
     def offset_of(slot):
-        partner = lax.rem(fragment + reach_ref[slot], fragments)
-        return [anchors_ref[partner, i] - anchors_ref[fragment, i] for i in range(3)]
+        partner = lax.rem(fragment + reach_of(slot), fragments)
+        return [anchor(partner, i) - anchor(fragment, i) for i in range(3)]
+
+    def steps(count, body, most):
+        width = max(n for n in range(1, most + 1) if count % n == 0)
+
+        def step(i, _):
+            for j in range(width):
+                body(i * width + j)
+            return 0
+
+        if width == count:
+            step(0, 0)
+        else:
+            lax.fori_loop(0, count // width, step, 0)
 
     def columns(k):
         return pl.ds(pl.multiple_of(k * LANES, LANES), LANES)
@@ -426,8 +451,10 @@
         out = []
         for i in range(count):
             value = jnp.where(lane < LANES - part, pieces[i], pieces[i + 1])
-            y = spots_ref[0, pl.ds(k + i, 1), :] - delta[1]
-            z = spots_ref[1, pl.ds(k + i, 1), :] - delta[2]
+            spot = (k + i) * LANES + lax.broadcasted_iota(jnp.int32, (1, LANES), 1)
+            y = ((spot.astype(jnp.float32) + 0.5) * (1.0 / edge)).astype(jnp.int32)
+            z = spot - y * edge - delta[2]
+            y = y - delta[1]
             inside = (y >= 0) & (y < edge) & (z >= 0) & (z < edge)
             out.append(jnp.where(inside & rows_inside, value, 0.0))
         return out
@@ -442,27 +469,25 @@
         offsets = [offset_of(slot) for slot, _ in picked]
         weights = [live.astype(jnp.float32) for _, live in picked]
 
-        def widen(g, _):
+        def widen(g):
             for side in range(2):
                 for i in range(stretch):
                     k = g * stretch + i
                     wide[side, k, middle, :] = far[side, :, columns(k)]
-            return 0
-
-        lax.fori_loop(0, chunks // stretch, widen, 0)
-
-        def make_density(g, _):
+
+        steps(chunks // stretch, widen, 3)
+
+        def make_density(g):
             for side in range(2):
                 values = shifted(wide.at[side], offsets[side], g * stretch, stretch)
                 for i, value in enumerate(values):
                     k = g * stretch + i
                     moved[side, k] = value
                     dense[side, k, middle, :] = weights[side] * near[side, :, columns(k)] * value
-            return 0
-
-        lax.fori_loop(0, chunks // stretch, make_density, 0)
-
-        def spread(g, _):
+
+        steps(chunks // stretch, make_density, 3)
+
+        def spread(g):
             parts = [
                 [dense[side, g * group_chunks + q, middle, :] for q in range(group_chunks)]
                 for side in range(2)
@@ -481,9 +506,8 @@
                     sides.append(value)
                 at = pl.multiple_of((g * period + i) * edge, ROWS)
                 cube[pl.ds(at, edge), :] = jnp.where(lane < HALF, sides[0], sides[1])
-            return 0
-
-        lax.fori_loop(0, edge // period, spread, 0)
+
+        steps(edge // period, spread, 2)
 
         def tile(t, i, size):
             return pl.ds(pl.multiple_of(i * size + t * ROWS, ROWS), ROWS)
@@ -491,7 +515,7 @@
         def across(t, i, size):
             return pl.ds(t * (ROWS * size) + i, ROWS, stride=size)
 
-        def over_y(t, _):
+        def over_y(t):
             values = real_dft([Number(cube[tile(t, i, edge), :]) for i in range(edge)])
             for i in range(half):
                 at = tile(t, i, edge)
@@ -499,56 +523,51 @@
                 lower[1, at, :] = (
                     jnp.zeros((ROWS, LANES), jnp.float32) if values[i].imag is None else values[i].imag
                 )
-            return 0
-
-        lax.fori_loop(0, tiles, over_y, 0)
-
-        def over_x(t, _):
+
+        steps(tiles, over_y, 3)
+
+        def over_x(t):
             at = [across(t, i, edge) for i in range(edge)]
             values = dft([Number(lower[0, a, :], lower[1, a, :]) for a in at], -1)
             for i in range(edge):
                 upper[0, tile(t, i, height), :] = values[i].real
                 upper[1, tile(t, i, height), :] = values[i].imag
-            return 0
-
-        lax.fori_loop(0, height // ROWS, over_x, 0)
+
+        steps(height // ROWS, over_x, 2)
 
         block = next(n for n in (512, 256, 128, 64, 32, 16, 8) if edge * height % n == 0)
 
-        def screen(c, _):
+        def screen(c):
             at = pl.ds(pl.multiple_of(c * block, block), block)
             real, imag = split_dot(upper[0, at, :], upper[1, at, :], ahead_ref)
             factor = screen_ref[at, :]
             real, imag = split_dot(real * factor, imag * factor, behind_ref)
             upper[0, at, :] = real
             upper[1, at, :] = imag
-            return 0
-
-        lax.fori_loop(0, edge * height // block, screen, 0)
-
-        def back_x(t, _):
+
+        steps(edge * height // block, screen, 3)
+
+        def back_x(t):
             at = [tile(t, i, height) for i in range(edge)]
             values = dft([Number(upper[0, a, :], upper[1, a, :]) for a in at], 1)
             for i in range(edge):
                 upper[0, at[i], :] = values[i].real
                 upper[1, at[i], :] = values[i].imag
-            return 0
-
-        lax.fori_loop(0, height // ROWS, back_x, 0)
-
-        def back_y(t, _):
+
+        steps(height // ROWS, back_x, 2)
+
+        def back_y(t):
             at = [across(t, i, height) for i in range(half)]
             values = [Number(upper[0, a, :], upper[1, a, :]) for a in at]
             values = values + [values[edge - i].conj() for i in range(half, edge)]
             for i, value in enumerate(real_back(values)):
                 cube[tile(t, i, edge), :] = value
-            return 0
-
-        lax.fori_loop(0, tiles, back_y, 0)
-
-        firsts = [first_ref[slot] for slot, _ in picked]
-
-        def collect(g, _):
+
+        steps(tiles, back_y, 3)
+
+        firsts = [first_of(slot) for slot, _ in picked]
+
+        def collect(g):
             planes = [
                 cube[pl.ds(pl.multiple_of((g * period + i) * edge, ROWS), edge), :]
                 for i in range(period)
@@ -570,26 +589,24 @@
                     for t in range(tiles):
                         at = pl.ds(t * (ROWS * chunks) + k, ROWS, stride=chunks)
                         act[firsts[side], at, :] += forward[t * ROWS : (t + 1) * ROWS]
-            return 0
-
-        lax.fori_loop(0, edge // period, collect, 0)
+
+        steps(edge // period, collect, 2)
 
         homes = []
         for side in range(2):
             slot = picked[side][0]
-            homes.append(reach_ref[slot] * orb_dev + lax.rem(second_ref[slot], orb_dev))
+            homes.append(reach_of(slot) * orb_dev + lax.rem(second_of(slot), orb_dev))
         returns = [[-d for d in delta] for delta in offsets]
 
-        def send_back(g, _):
+        def send_back(g):
             for side in range(2):
                 values = shifted(dense.at[side], returns[side], g * stretch, stretch)
                 for i, value in enumerate(values):
                     for t in range(tiles):
                         at = pl.ds(t * (ROWS * chunks) + g * stretch + i, ROWS, stride=chunks)
                         back[homes[side], at, :] += value[t * ROWS : (t + 1) * ROWS]
-            return 0
-
-        lax.fori_loop(0, chunks // stretch, send_back, 0)
+
+        steps(chunks // stretch, send_back, 3)
         return 0
 
     lax.fori_loop(0, lax.div(found + 1, 2), solve_two, 0)
@@ -622,24 +639,20 @@
     return sum(((k >> i) & 1) << (bits - 1 - i) for i in range(bits))
 
 
-def pair_terms(places, pair_count, pair_first, pair_second, pair_reach, anchors, screen, pieces, far):
+def pair_terms(numbers, fragments, slots, screen, pieces, far):
     orb_dev, edge, plane = pieces[0].shape
     groups = len(pieces)
     frag_size = groups * orb_dev
-    fragments = anchors.shape[0]
-    slots = pair_first.shape[0]
     chunks = plane // LANES
     rows = edge * chunks
     height = padded_half(edge)
     returns_count = (REACH + 1) * orb_dev
-    spots = np.arange(plane, dtype=np.int32).reshape(chunks, LANES)
-    spots = jnp.asarray(np.stack([spots // edge, spots % edge]))
     ahead, behind = lane_matrices(edge)
     shape = (edge, orb_dev, groups, fragments, slots)
     smem = pl.BlockSpec(memory_space=pltpu.SMEM)
     hbm = pl.BlockSpec(memory_space=pltpu.HBM)
     f32 = jnp.float32
-    tables = [spots, screen, jnp.asarray(ahead), jnp.asarray(behind)]
+    tables = [screen, jnp.asarray(ahead), jnp.asarray(behind)]
     found = pl.pallas_call(
         functools.partial(pair_kernel, shape),
         out_shape=[jax.ShapeDtypeStruct((groups // 2, frag_size, rows // groups, LANES), f32)] * 2
@@ -647,7 +660,7 @@
             jax.ShapeDtypeStruct((count, rows, LANES), f32)
             for count in (1, orb_dev - 1, orb_dev, orb_dev)
         ],
-        in_specs=[smem] * 6 + [hbm] * (4 + groups + len(far)),
+        in_specs=[smem] + [hbm] * (3 + groups + len(far)),
         out_specs=[hbm] * 6,
         scratch_shapes=[
             pltpu.VMEM((frag_size, rows, LANES), f32),
@@ -664,14 +677,11 @@
             pltpu.SemaphoreType.DMA((2, 2)),
             pltpu.SemaphoreType.DMA((groups + 4,)),
             *[pltpu.VMEM(table.shape, table.dtype) for table in tables],
-            pltpu.SemaphoreType.DMA((4,)),
+            pltpu.SemaphoreType.DMA((3,)),
         ],
         compiler_params=pltpu.CompilerParams(vmem_limit_bytes=40 << 20),
         name="pair_terms",
-    )(
-        places, pair_count, pair_first, pair_second, pair_reach, anchors,
-        *tables, *pieces, *far,
-    )
+    )(numbers, *tables, *pieces, *far)
     return found[:2], found[2:]
 
 
@@ -864,6 +874,10 @@
     return gradient.transpose(1, 0, 2), lagrange
 
 
+def together(*arrays):
+    return lax.optimization_barrier(arrays)
+
+
 def to_fragment(block, distance, senders=None):
     devices = lax.axis_size("orb")
     senders = range(devices) if senders is None else range(senders, devices, 2)
@@ -883,7 +897,8 @@
     orb_dev, edge, plane = orbitals.shape
     frag_size = groups * orb_dev
     places = jnp.stack([lax.axis_index("orb"), lax.axis_index("grp")]).astype(jnp.int32)
-    screen = screen_terms(kernel)
+    numbers = [places, pair_count, pair_first, pair_second, pair_reach, anchors.reshape(-1)]
+    screen, numbers = screen_terms(jnp.concatenate(numbers), kernel)
 
     two = to_fragment(orbitals, -2)
     twin = with_twin(orbitals[:1])
@@ -894,23 +909,23 @@
     while bit:
         for k in list(pieces):
             pieces[k ^ bit] = with_member(pieces[k], bit)
+        if bit == groups // 2:
+            pieces[bit], one = together(pieces[bit], one)
         bit //= 2
     pieces = [pieces[k] for k in range(groups)]
 
     (kept, sent), (back_first, back_rest, back_two, own) = pair_terms(
-        places, pair_count, pair_first, pair_second, pair_reach, anchors, screen,
-        pieces, [twin, relay, one, two],
+        numbers, anchors.shape[0], pair_first.shape[0], screen, pieces, [twin, relay, one, two]
     )
 
     two = to_fragment(back_two, 2)
-    twin = with_twin(back_first)
     one = to_fragment(back_rest, 1)
-    relay = to_fragment(twin, 2, 0)
-
     bit = 1
     arrived = [with_member(sent, bit)]
     while 2 * bit < groups:
         kept = kept + jnp.concatenate(arrived, axis=1)
+        if bit == 1:
+            kept, back_first = together(kept, back_first)
         half = kept.shape[0] // 2
         cut = frag_size // orb_dev
         bit *= 2
@@ -918,6 +933,8 @@
             with_member(kept[half:, i : i + cut], bit) for i in range(0, frag_size, cut)
         ]
         kept = kept[:half]
+    twin = with_twin(back_first)
+    relay = to_fragment(twin, 2, 0)
 
     flat, phi = flatten_terms(places, pieces)
     act, parcels = home_terms(places, edge, flat, phi, kept, arrived, own, twin, relay, one, two)

time: 119 us -> 114 us (0.958); the launches traced: 119 us -> 116 us
  waiting for transfers between devices: 54.2 us -> 51 us
    ppermute x10, waiting for transfers between devices: 34.2 us -> 15.8 us  [with_member(): lax.ppermute(block, 'grp', [(i, i ^ bit) for i in range(lax.axis_size('gr...]
    ppermute x6, waiting for transfers between devices: 9.67 us -> 26.9 us  [to_fragment(): lax.ppermute(block, 'orb', [(i, (i + distance) % devices) for i in senders])]
    ppermute x2, starting transfers between devices: 3.38 us -> 7.26 us  [with_twin(): lax.ppermute(block, 'orb', [(i, i ^ 1) for i in range(lax.axis_size('orb'...]
    ppermute x6, starting transfers between devices: 12.5 us -> 9.7 us  [to_fragment(): lax.ppermute(block, 'orb', [(i, (i + distance) % devices) for i in senders])]
    ppermute x2, waiting for transfers between devices: 10.3 us -> 8.24 us  [with_twin(): lax.ppermute(block, 'orb', [(i, i ^ 1) for i in range(lax.axis_size('orb'...]
    pallas_call x1, Pallas kernels: 12.6 us -> 11.2 us  [pair_terms(): pl.pallas_call(functools.partial(pair_kernel, shape), out_shape=[jax.Shap...]
    unnamed x21 -> x23, local copies, waits for them, and re-layouts: 5.99 us -> 6.46 us
  transfers between devices with their start and end apart: 18 -> 18, of which waited for: 9 -> 9; matrix products, arithmetic and copies ran while one was open for 3% -> 2% of each run, Pallas kernels for 3% -> 4%
where the time goes in v1:
time: 114 us; the launch traced here: 116 us
  waiting for transfers between devices  51 us (45%)
  starting transfers between devices  33.5 us (29%)
  Pallas kernels  21.3 us (19%)
  local copies, waits for them, and re-layouts  8.6 us (8%)
  between operations  1.45 us (1%)
    ppermute x6, waiting for transfers between devices, to_fragment(): lax.ppermute(block, 'orb', [(i, (i + distance) % devices) for i in senders])  26.9 us
    ppermute x10, starting transfers between devices, with_member(): lax.ppermute(block, 'grp', [(i, i ^ bit) for i in range(lax.axis_size('gr...  16.5 us
    ppermute x10, waiting for transfers between devices, with_member(): lax.ppermute(block, 'grp', [(i, i ^ bit) for i in range(lax.axis_size('gr...  15.8 us
    pallas_call x1, Pallas kernels, pair_terms(): pl.pallas_call(functools.partial(pair_kernel, shape), out_shape=[jax.Shap...  11.2 us
    ppermute x6, starting transfers between devices, to_fragment(): lax.ppermute(block, 'orb', [(i, (i + distance) % devices) for i in senders])  9.7 us
    ppermute x2, waiting for transfers between devices, with_twin(): lax.ppermute(block, 'orb', [(i, i ^ 1) for i in range(lax.axis_size('orb'...  8.24 us
    ppermute x2, starting transfers between devices, with_twin(): lax.ppermute(block, 'orb', [(i, i ^ 1) for i in range(lax.axis_size('orb'...  7.26 us
    unnamed x23, local copies, waits for them, and re-layouts  6.46 us
  transfers between devices with their start and end apart: 18, of which 9 were waited for; matrix products, arithmetic and copies ran while one was open for 2% of the time, Pallas kernels for 4%

profile of v1, /device:TPU:0, one launch (start us, length us, event | category | flops | bytes accessed | tf_op | source)
XLA Modules:
  0.0 116.1 jit_solution(12778687922700739044)
XLA Ops:
  0.7 3.0 %collective-permute-start.1 = (f32[2,48,2304]{2,1,0:T(8,128)}, f32[2,48,2304]{2,1,0:T(8,128)S(1)}, u32[]{:S(2)}, u32[]{:S(2)}) collective-permute-start(f32[2,48,2304]{2,1,0:T(8,128)} %refs_3_.1), channel_id=1, source_target_pairs={{0,2},{1,3},{2,0},{3,1},{4,6},{5,7},{6,4},{7,5},{8,10},{9,11},{10,... | collective-permute-start | bytes 2654216 | tf_op jit(solution)/shard_map/ppermute | solution.py:892
  3.7 1.2 %fusion.1 = (f32[1,48,2304]{2,1,0:T(8,128)S(1)}, f32[1,48,2304]{2,1,0:T(8,128)S(1)}) fusion(f32[2,48,2304]{2,1,0:T(8,128)} %refs_3_.1), kind=kLoop, calls=%fused_computation.2 | loop fusion | bytes 1769472 | tf_op jit(solution)/shard_map/slice | solution.py:904
  4.9 4.6 %collective-permute-start.2 = (f32[1,48,2304]{2,1,0:T(8,128)S(1)}, f32[1,48,2304]{2,1,0:T(8,128)S(1)}, u32[]{:S(2)}, u32[]{:S(2)}) collective-permute-start(f32[1,48,2304]{2,1,0:T(8,128)S(1)} %get-tuple-element.47), channel_id=1, source_target_pairs={{0,28},{4,0},{8,4},{12,8},{16,12},{20,16},{24,20},{28,24},{1,29},{... | collective-permute-start | bytes 1327112 | tf_op jit(solution)/shard_map/ppermute | solution.py:884
  9.9 0.6 collective-permute-start.4
  10.6 9.5 %collective-permute-done.2.refs_9_ = f32[1,48,2304]{2,1,0:T(8,128)S(1)} collective-permute-done((f32[1,48,2304]{2,1,0:T(8,128)S(1)}, f32[1,48,2304]{2,1,0:T(8,128)S(1)}, u32[]{:S(2)}, u32[]{:S(2)}) %collective-permute-start.2) | collective-permute-done | bytes 442400 | tf_op jit(solution)/shard_map/ppermute | solution.py:884
  20.1 0.8 copy-done.2
  20.9 2.7 %collective-permute-done.1.refs_2_.refs_5_ = f32[2,48,2304]{2,1,0:T(8,128)S(1)} collective-permute-done((f32[2,48,2304]{2,1,0:T(8,128)}, f32[2,48,2304]{2,1,0:T(8,128)S(1)}, u32[]{:S(2)}, u32[]{:S(2)}) %collective-permute-start.1) | collective-permute-done | bytes 884768 | tf_op jit(solution)/shard_map/ppermute | solution.py:892
  23.6 2.6 %collective-permute-done.4.refs_7_ = f32[1,48,2304]{2,1,0:T(8,128)} collective-permute-done((f32[1,48,2304]{2,1,0:T(8,128)S(1)}, f32[1,48,2304]{2,1,0:T(8,128)}, u32[]{:S(2)}, u32[]{:S(2)}) %collective-permute-start.4) | collective-permute-done | bytes 442400 | tf_op jit(solution)/shard_map/ppermute | solution.py:888
  26.2 1.4 %collective-permute-start.5 = (f32[1,48,2304]{2,1,0:T(8,128)}, f32[1,48,2304]{2,1,0:T(8,128)}, u32[]{:S(2)}, u32[]{:S(2)}) collective-permute-start(f32[1,48,2304]{2,1,0:T(8,128)} %collective-permute-done.4.refs_7_), channel_id=1, source_target_pairs={{4,28},{12,4},{20,12},{28,20},{5,29},{13,5},{21,13},{29,21},{6,30}... | collective-permute-start | bytes 1327112 | tf_op jit(solution)/shard_map/ppermute | solution.py:884
  28.5 0.7 concatenate.4.numbers_ref
  29.2 1.0 copy-done.1
  30.2 0.8 copy-done.6
  31.1 0.7 copy-done.7
  31.8 3.5 %screen_terms.1 = (f32[1536,128]{1,0:T(8,128)S(1)}, s32[51]{0:T(128)S(1)}) custom-call(s32[51]{0:T(128)S(1)} %concatenate.4.numbers_ref, f32[48,2304]{1,0:T(8,128)S(1)} %copy-done.1, f32[48,48]{1,0:T(8,128)S(1)} %copy-done.7, f32[128,128]{1,0:T(8,128)S(1)} %copy-done.6), custom_call_target="tpu_custom_call" | custom-call | tf_op jit(solution)/shard_map/screen_terms/pallas_call | solution.py:293
  35.3 2.3 %collective-permute-done.6.refs_10_ = f32[2,48,2304]{2,1,0:T(8,128)} collective-permute-done((f32[2,48,2304]{2,1,0:T(8,128)S(1)}, f32[2,48,2304]{2,1,0:T(8,128)}, u32[]{:S(2)}, u32[]{:S(2)}) %collective-permute-start.6) | collective-permute-done | bytes 884768 | tf_op jit(solution)/shard_map/ppermute | solution.py:884
  37.6 1.0 copy-done.3
  38.6 1.0 copy-done.4
  39.6 1.0 copy-done.5
  40.6 11.2 %pair_terms.1 = (f32[2,8,216,128]{3,2,1,0:T(8,128)S(1)}, f32[2,8,216,128]{3,2,1,0:T(8,128)S(1)}, f32[1,864,128]{2,1,0:T(8,128)S(1)}, f32[1,864,128]{2,1,0:T(8,12...) custom-call(s32[51]{0:T(128)S(1)} %get-tuple-element.26.numbers_ref, ...), custom_call_target="tpu_custom_call" | custom-call | tf_op jit(solution)/shard_map/pair_terms/pallas_call | solution.py:656
  51.8 0.8 collective-permute-start.13
  52.6 2.9 %collective-permute-done.7 = f32[2,8,216,128]{3,2,1,0:T(8,128)S(1)} collective-permute-done((f32[2,8,216,128]{3,2,1,0:T(8,128)S(1)}, f32[2,8,216,128]{3,2,1,0:T(8,128)S(1)}, u32[]{:S(2)}, u32[]{:S(2)}) %collective-permute-start.7) | collective-permute-done | bytes 1769504 | tf_op jit(solution)/shard_map/ppermute | solution.py:892
  55.7 6.6 %collective-permute-start.10 = (f32[1,864,128]{2,1,0:T(8,128)S(1)}, f32[1,864,128]{2,1,0:T(8,128)S(1)}, u32[]{:S(2)}, u32[]{:S(2)}) collective-permute-start(f32[1,864,128]{2,1,0:T(8,128)S(1)} %get-tuple-element.34), channel_id=1, source_target_pairs={{0,4},{4,0},{8,12},{12,8},{16,20},{20,16},{24,28},{28,24},{1,5},{5... | collective-permute-start | bytes 1327112 | tf_op jit(solution)/shard_map/ppermute | solution.py:888
  62.4 4.7 %collective-permute-start.8 = (f32[1,4,216,128]{3,2,1,0:T(8,128)S(1)}, f32[1,4,216,128]{3,2,1,0:T(8,128)S(1)}, u32[]{:S(2)}, u32[]{:S(2)}) collective-permute-start(f32[1,4,216,128]{3,2,1,0:T(8,128)S(1)} %get-tuple-element.45), channel_id=1, source_target_pairs={{0,2},{1,3},{2,0},{3,1},{4,6},{5,7},{6,4},{7,5},{8,10},{9,11},{10,... | collective-permute-start | bytes 1327112 | tf_op jit(solution)/shard_map/ppermute | solution.py:892
  67.2 5.6 %collective-permute-done.10.refs_3_ = f32[1,864,128]{2,1,0:T(8,128)S(1)} collective-permute-done((f32[1,864,128]{2,1,0:T(8,128)S(1)}, f32[1,864,128]{2,1,0:T(8,128)S(1)}, u32[]{:S(2)}, u32[]{:S(2)}) %collective-permute-start.10) | collective-permute-done | bytes 442400 | tf_op jit(solution)/shard_map/ppermute | solution.py:888
  72.8 2.4 %collective-permute-start.11 = (f32[1,864,128]{2,1,0:T(8,128)S(1)}, f32[1,864,128]{2,1,0:T(8,128)S(1)}, u32[]{:S(2)}, u32[]{:S(2)}) collective-permute-start(f32[1,864,128]{2,1,0:T(8,128)S(1)} %collective-permute-done.10.refs_3_), channel_id=1, source_target_pairs={{0,8},{8,16},{16,24},{24,0},{1,9},{9,17},{17,25},{25,1},{2,10},{10... | collective-permute-start | bytes 1327112 | tf_op jit(solution)/shard_map/ppermute | solution.py:884
  75.3 1.5 %flatten_terms.1 = (f32[8,864,128]{2,1,0:T(8,128)S(1)}, f32[8,216,128]{2,1,0:T(8,128)S(1)}) custom-call(s32[2]{0:T(128)S(1)} %pad_add_fusion.places_ref, f32[2,48,2304]{2,1,0:T(8,128)S(1)} %copy-done, f32[2,48,2304]{2,1,0:T(8,128)S(1)} %collective-permute-done.refs_1_.refs_4_, f32[2,48,2304]{2,1,0:T(8,128)S(1)} %collective-permute-done.1.refs_2_.refs_5_, ...), custom_call_target="tpu_custom_call" | custom-call | tf_op jit(solution)/shard_map/flatten_terms/pallas_call | solution.py:714
  76.9 15.1 %collective-permute-done.12.refs_5_ = f32[1,864,128]{2,1,0:T(8,128)S(1)} collective-permute-done((f32[1,864,128]{2,1,0:T(8,128)S(1)}, f32[1,864,128]{2,1,0:T(8,128)S(1)}, u32[]{:S(2)}, u32[]{:S(2)}) %collective-permute-start.12) | collective-permute-done | bytes 442400 | tf_op jit(solution)/shard_map/ppermute | solution.py:884
  92.0 2.4 %home_terms.1 = (f32[8,216,128]{2,1,0:T(8,128)S(1)}, f32[440,128]{1,0:T(8,128)S(1)}, f32[440,128]{1,0:T(8,128)S(1)}, f32[440,128]{1,0:T(8,128)S(1)}, f32[440,128]{1,0:T(8,128)S(1)}) custom-call(s32[2]{0:T(128)S(1)} %pad_add_fusion.places_ref, f32[8,864,128]{2,1,0:T(8,128)S(1)} %get-tuple-element.24.flat_ref, f32[8,216,128]{2,1,0:T(8,128)S(1)} %get-tuple-element.25.phi_ref, ...), custom_call_target="tpu_custom_call" | custom-call | tf_op jit(solution)/shard_map/home_terms/pallas_call | solution.py:807
  94.5 8.5 %collective-permute-start.16 = (f32[440,128]{1,0:T(8,128)S(1)}, f32[440,128]{1,0:T(8,128)S(1)}, u32[]{:S(2)}, u32[]{:S(2)}) collective-permute-start(f32[440,128]{1,0:T(8,128)S(1)} %get-tuple-element.41), channel_id=1, source_target_pairs={{0,2},{1,3},{2,0},{3,1},{4,6},{5,7},{6,4},{7,5},{8,10},{9,11},{10,... | collective-permute-start | bytes 675848 | tf_op jit(solution)/shard_map/ppermute | solution.py:892
  103.1 6.2 %collective-permute-done.16 = f32[440,128]{1,0:T(8,128)S(1)} collective-permute-done((f32[440,128]{1,0:T(8,128)S(1)}, f32[440,128]{1,0:T(8,128)S(1)}, u32[]{:S(2)}, u32[]{:S(2)}) %collective-permute-start.16) | collective-permute-done | bytes 225312 | tf_op jit(solution)/shard_map/ppermute | solution.py:892
  109.3 4.0 %collective-permute-done.15.refs_2_ = f32[440,128]{1,0:T(8,128)S(1)} collective-permute-done((f32[440,128]{1,0:T(8,128)S(1)}, f32[440,128]{1,0:T(8,128)S(1)}, u32[]{:S(2)}, u32[]{:S(2)}) %collective-permute-start.15) | collective-permute-done | bytes 225312 | tf_op jit(solution)/shard_map/ppermute | solution.py:892
  113.3 2.8 %gradient_terms.1 = (f32[12,8,2304]{2,1,0:T(8,128)}, f32[8,8]{1,0:T(8,128)}) custom-call(s32[2]{0:T(128)S(1)} %pad_add_fusion.places_ref, f32[8,216,128]{2,1,0:T(8,128)S(1)} %get-tuple-element.37.act_ref, f32[8,216,128]{2,1,0:T(8,128)S(1)} %get-tuple-element.25.phi_ref, f32[440,128]{1,0:T(8,128)S(1)} %get-tuple-element.38.refs_0_, ...), custom_call_target="tpu_custom_call" | custom-call | tf_op jit(solution)/shard_map/gradient_terms/pallas_call | solution.py:859
  (39 shorter events, 1.4 us)
Async XLA Ops:
  0.6 8.9 %copy-start = (f32[2,48,2304]{2,1,0:T(8,128)S(1)}, f32[2,48,2304]{2,1,0:T(8,128)}, u32[]{:S(2)}) copy-start(f32[2,48,2304]{2,1,0:T(8,128)} %refs_3_.1) | copy-start | bytes 2654212
  0.6 27.0 %copy-start.8 = (s32[8,3]{0,1:T(4,128)S(1)}, s32[8,3]{0,1:T(4,128)}, u32[]{:S(2)}) copy-start(s32[8,3]{0,1:T(4,128)} %param.13) | copy-start | bytes 292
  0.7 27.8 %copy-start.9 = (s32[8]{0:T(128)S(1)}, s32[8]{0:T(128)}, u32[]{:S(2)}) copy-start(s32[8]{0:T(128)} %param.15) | copy-start | bytes 100
  0.7 27.8 %copy-start.10 = (s32[8]{0:T(128)S(1)}, s32[8]{0:T(128)}, u32[]{:S(2)}) copy-start(s32[8]{0:T(128)} %param.16) | copy-start | bytes 100
  0.7 22.9 %collective-permute-start.1 = (f32[2,48,2304]{2,1,0:T(8,128)}, f32[2,48,2304]{2,1,0:T(8,128)S(1)}, u32[]{:S(2)}, u32[]{:S(2)}) collective-permute-start(f32[2,48,2304]{2,1,0:T(8,128)} %refs_3_.1), channel_id=1, source_target_pairs={{0,2},{1,3},{2,0},{3,1},{4,6},{5,7},{6,4},{7,5},{8,10},{9,11},{10,... | collective-permute-start | bytes 2654216 | tf_op jit(solution)/shard_map/ppermute | solution.py:892
  4.9 15.2 %collective-permute-start.2 = (f32[1,48,2304]{2,1,0:T(8,128)S(1)}, f32[1,48,2304]{2,1,0:T(8,128)S(1)}, u32[]{:S(2)}, u32[]{:S(2)}) collective-permute-start(f32[1,48,2304]{2,1,0:T(8,128)S(1)} %get-tuple-element.47), channel_id=1, source_target_pairs={{0,28},{4,0},{8,4},{12,8},{16,12},{20,16},{24,20},{28,24},{1,29},{... | collective-permute-start | bytes 1327112 | tf_op jit(solution)/shard_map/ppermute | solution.py:884
  9.5 25.8 %collective-permute-start = (f32[2,48,2304]{2,1,0:T(8,128)S(1)}, f32[2,48,2304]{2,1,0:T(8,128)S(1)}, u32[]{:S(2)}, u32[]{:S(2)}) collective-permute-start(f32[2,48,2304]{2,1,0:T(8,128)S(1)} %copy-done), channel_id=1, source_target_pairs={{0,1},{1,0},{2,3},{3,2},{4,5},{5,4},{6,7},{7,6},{8,9},{9,8},{10,11... | collective-permute-start | bytes 2654216 | tf_op jit(solution)/shard_map/ppermute | solution.py:892
  9.5 28.1 %collective-permute-start.6 = (f32[2,48,2304]{2,1,0:T(8,128)S(1)}, f32[2,48,2304]{2,1,0:T(8,128)}, u32[]{:S(2)}, u32[]{:S(2)}) collective-permute-start(f32[2,48,2304]{2,1,0:T(8,128)S(1)} %copy-done), channel_id=1, source_target_pairs={{0,24},{4,28},{8,0},{12,4},{16,8},{20,12},{24,16},{28,20},{1,25},{... | collective-permute-start | bytes 2654216 | tf_op jit(solution)/shard_map/ppermute | solution.py:884
  9.9 16.2 %collective-permute-start.4 = (f32[1,48,2304]{2,1,0:T(8,128)S(1)}, f32[1,48,2304]{2,1,0:T(8,128)}, u32[]{:S(2)}, u32[]{:S(2)}) collective-permute-start(f32[1,48,2304]{2,1,0:T(8,128)S(1)} %get-tuple-element.46), channel_id=1, source_target_pairs={{0,4},{4,0},{8,12},{12,8},{16,20},{20,16},{24,28},{28,24},{1,5},{5... | collective-permute-start | bytes 1327112 | tf_op jit(solution)/shard_map/ppermute | solution.py:888
  20.1 0.8 copy-start.2
  23.6 14.0 %collective-permute-start.3 = (f32[2,48,2304]{2,1,0:T(8,128)S(1)}, f32[2,48,2304]{2,1,0:T(8,128)S(1)}, u32[]{:S(2)}, u32[]{:S(2)}) collective-permute-start(f32[2,48,2304]{2,1,0:T(8,128)S(1)} %collective-permute-done.1.refs_2_.refs_5_), channel_id=1, source_target_pairs={{0,1},{1,0},{2,3},{3,2},{4,5},{5,4},{6,7},{7,6},{8,9},{9,8},{10,11... | collective-permute-start | bytes 2654216 | tf_op jit(solution)/shard_map/ppermute | solution.py:892
  26.2 9.1 %collective-permute-start.5 = (f32[1,48,2304]{2,1,0:T(8,128)}, f32[1,48,2304]{2,1,0:T(8,128)}, u32[]{:S(2)}, u32[]{:S(2)}) collective-permute-start(f32[1,48,2304]{2,1,0:T(8,128)} %collective-permute-done.4.refs_7_), channel_id=1, source_target_pairs={{4,28},{12,4},{20,12},{28,20},{5,29},{13,5},{21,13},{29,21},{6,30}... | collective-permute-start | bytes 1327112 | tf_op jit(solution)/shard_map/ppermute | solution.py:884
  29.2 1.0 copy-start.1
  30.2 0.8 copy-start.6
  31.1 0.7 copy-start.7
  37.6 1.0 copy-start.3
  38.6 1.0 copy-start.4
  39.6 1.0 copy-start.5
  51.8 3.8 %collective-permute-start.7 = (f32[2,8,216,128]{3,2,1,0:T(8,128)S(1)}, f32[2,8,216,128]{3,2,1,0:T(8,128)S(1)}, u32[]{:S(2)}, u32[]{:S(2)}) collective-permute-start(f32[2,8,216,128]{3,2,1,0:T(8,128)S(1)} %get-tuple-element.30), channel_id=1, source_target_pairs={{0,1},{1,0},{2,3},{3,2},{4,5},{5,4},{6,7},{7,6},{8,9},{9,8},{10,11... | collective-permute-start | bytes 5308424 | tf_op jit(solution)/shard_map/ppermute | solution.py:892
  51.8 40.2 %collective-permute-start.13 = (f32[2,864,128]{2,1,0:T(8,128)S(1)}, f32[2,864,128]{2,1,0:T(8,128)S(1)}, u32[]{:S(2)}, u32[]{:S(2)}) collective-permute-start(f32[2,864,128]{2,1,0:T(8,128)S(1)} %get-tuple-element.36), channel_id=1, source_target_pairs={{0,8},{4,12},{8,16},{12,20},{16,24},{20,28},{24,0},{28,4},{1,9},{5... | collective-permute-start | bytes 2654216 | tf_op jit(solution)/shard_map/ppermute | solution.py:884
  55.7 17.1 %collective-permute-start.10 = (f32[1,864,128]{2,1,0:T(8,128)S(1)}, f32[1,864,128]{2,1,0:T(8,128)S(1)}, u32[]{:S(2)}, u32[]{:S(2)}) collective-permute-start(f32[1,864,128]{2,1,0:T(8,128)S(1)} %get-tuple-element.34), channel_id=1, source_target_pairs={{0,4},{4,0},{8,12},{12,8},{16,20},{20,16},{24,28},{28,24},{1,5},{5... | collective-permute-start | bytes 1327112 | tf_op jit(solution)/shard_map/ppermute | solution.py:888
  62.3 29.7 %collective-permute-start.12 = (f32[1,864,128]{2,1,0:T(8,128)S(1)}, f32[1,864,128]{2,1,0:T(8,128)S(1)}, u32[]{:S(2)}, u32[]{:S(2)}) collective-permute-start(f32[1,864,128]{2,1,0:T(8,128)S(1)} %get-tuple-element.35), channel_id=1, source_target_pairs={{0,4},{4,8},{8,12},{12,16},{16,20},{20,24},{24,28},{28,0},{1,5},{5... | collective-permute-start | bytes 1327112 | tf_op jit(solution)/shard_map/ppermute | solution.py:884
  62.4 29.6 %collective-permute-start.8 = (f32[1,4,216,128]{3,2,1,0:T(8,128)S(1)}, f32[1,4,216,128]{3,2,1,0:T(8,128)S(1)}, u32[]{:S(2)}, u32[]{:S(2)}) collective-permute-start(f32[1,4,216,128]{3,2,1,0:T(8,128)S(1)} %get-tuple-element.45), channel_id=1, source_target_pairs={{0,2},{1,3},{2,0},{3,1},{4,6},{5,7},{6,4},{7,5},{8,10},{9,11},{10,... | collective-permute-start | bytes 1327112 | tf_op jit(solution)/shard_map/ppermute | solution.py:892
  67.1 24.9 %collective-permute-start.9 = (f32[1,4,216,128]{3,2,1,0:T(8,128)S(1)}, f32[1,4,216,128]{3,2,1,0:T(8,128)S(1)}, u32[]{:S(2)}, u32[]{:S(2)}) collective-permute-start(f32[1,4,216,128]{3,2,1,0:T(8,128)S(1)} %get-tuple-element.44), channel_id=1, source_target_pairs={{0,2},{1,3},{2,0},{3,1},{4,6},{5,7},{6,4},{7,5},{8,10},{9,11},{10,... | collective-permute-start | bytes 1327112 | tf_op jit(solution)/shard_map/ppermute | solution.py:892
  72.8 19.2 %collective-permute-start.11 = (f32[1,864,128]{2,1,0:T(8,128)S(1)}, f32[1,864,128]{2,1,0:T(8,128)S(1)}, u32[]{:S(2)}, u32[]{:S(2)}) collective-permute-start(f32[1,864,128]{2,1,0:T(8,128)S(1)} %collective-permute-done.10.refs_3_), channel_id=1, source_target_pairs={{0,8},{8,16},{16,24},{24,0},{1,9},{9,17},{17,25},{25,1},{2,10},{10... | collective-permute-start | bytes 1327112 | tf_op jit(solution)/shard_map/ppermute | solution.py:884
  94.5 14.8 %collective-permute-start.16 = (f32[440,128]{1,0:T(8,128)S(1)}, f32[440,128]{1,0:T(8,128)S(1)}, u32[]{:S(2)}, u32[]{:S(2)}) collective-permute-start(f32[440,128]{1,0:T(8,128)S(1)} %get-tuple-element.41), channel_id=1, source_target_pairs={{0,2},{1,3},{2,0},{3,1},{4,6},{5,7},{6,4},{7,5},{8,10},{9,11},{10,... | collective-permute-start | bytes 675848 | tf_op jit(solution)/shard_map/ppermute | solution.py:892
  103.0 6.3 %collective-permute-start.14 = (f32[440,128]{1,0:T(8,128)S(1)}, f32[440,128]{1,0:T(8,128)S(1)}, u32[]{:S(2)}, u32[]{:S(2)}) collective-permute-start(f32[440,128]{1,0:T(8,128)S(1)} %get-tuple-element.39), channel_id=1, source_target_pairs={{0,1},{1,0},{2,3},{3,2},{4,5},{5,4},{6,7},{7,6},{8,9},{9,8},{10,11... | collective-permute-start | bytes 675848 | tf_op jit(solution)/shard_map/ppermute | solution.py:892
  103.0 10.4 %collective-permute-start.15 = (f32[440,128]{1,0:T(8,128)S(1)}, f32[440,128]{1,0:T(8,128)S(1)}, u32[]{:S(2)}, u32[]{:S(2)}) collective-permute-start(f32[440,128]{1,0:T(8,128)S(1)} %get-tuple-element.40), channel_id=1, source_target_pairs={{0,2},{1,3},{2,0},{3,1},{4,6},{5,7},{6,4},{7,5},{8,10},{9,11},{10,... | collective-permute-start | bytes 675848 | tf_op jit(solution)/shard_map/ppermute | solution.py:892
  109.3 4.0 %collective-permute-start.17 = (f32[440,128]{1,0:T(8,128)S(1)}, f32[440,128]{1,0:T(8,128)S(1)}, u32[]{:S(2)}, u32[]{:S(2)}) collective-permute-start(f32[440,128]{1,0:T(8,128)S(1)} %collective-permute-done.16), channel_id=1, source_target_pairs={{0,1},{1,0},{2,3},{3,2},{4,5},{5,4},{6,7},{7,6},{8,9},{9,8},{10,11... | collective-permute-start | bytes 675848 | tf_op jit(solution)/shard_map/ppermute | solution.py:892
